TPU v7x, 128 devices: a whole 4x4x4 slice. The times are simulated.
128 devices in a mesh: seq: 4 (over y), slide: 32 (over x, z, core).
Axes of the slice: x: 4, y: 4, z: 4, core: 2. Of those that a mesh axis runs over, the one named last changes fastest.
Arguments:
- patches: bfloat16 [32, 4096, 768], P('slide', 'seq'), may hold values from -13 to 13
- w_query: bfloat16 [768, 768], replicated
- w_key: bfloat16 [768, 768], replicated
- w_value: bfloat16 [768, 768], replicated, may hold values from -0.21875 to 0.21875
- w_out: bfloat16 [768, 768], replicated, may hold values from -0.21875 to 0.21875
- lengths: int32 [32], P('slide'), may hold values from 512 to 4096, as said below
- cotangent: bfloat16 [32, 4096, 768], P('slide', 'seq'), may hold values from -6 to 6
Outputs:
- attended: bfloat16 [32, 4096, 768], P('slide', 'seq')
- grad_patches: bfloat16 [32, 4096, 768], P('slide', 'seq')
- grad_query: bfloat16 [768, 768], replicated
- grad_key: bfloat16 [768, 768], replicated
- grad_value: bfloat16 [768, 768], replicated
- grad_out: bfloat16 [768, 768], replicated
Inputs may be any that keep to these rules, and one draw needn't show every extreme that they name: The first lengths[s] positions of slide s are patches, the rest of its span is padding; some slide fills all 4096 positions.
All inputs are finite; a program needn't handle non-finite values.
Results may differ from a plain program's by a relative error of at most 0.025.
Values may be sent and summed in bfloat16 or wider, within the bound.
A program may use at most 192 MiB of HBM per device.

v0:
```python
import math

import jax
import jax.numpy as jnp
from jax import lax
from jax.sharding import PartitionSpec as P

ATTENTION_HEADS = 12
SEGMENT = 1024
FAR_DILATION = 4


NEGATIVE = -1e30


def pick_rows(block_span, head_total_count):
    leading_shape = block_span.shape[:-2]
    total_row_count, feature_channel_width = block_span.shape[-2:]
    head_feature_width = feature_channel_width // head_total_count
    memory_layout = block_span.reshape(
        leading_shape
        + (total_row_count // FAR_DILATION, FAR_DILATION, head_total_count, head_feature_width)
    )
    chosen_tokens = [
        memory_layout[..., segment_member % FAR_DILATION, segment_member, :]
        for segment_member in range(head_total_count)
    ]
    return jnp.stack(chosen_tokens, axis=-2).reshape(
        leading_shape + (total_row_count // FAR_DILATION, feature_channel_width)
    )


def place_rows(chosen_tokens, head_total_count):
    selected_count, feature_channel_width = chosen_tokens.shape
    head_feature_width = feature_channel_width // head_total_count
    selection_mask = (
        jnp.arange(FAR_DILATION)[:, None] == (jnp.arange(head_total_count) % FAR_DILATION)[None, :]
    ).astype(chosen_tokens.dtype)
    dilation_spread = (
        chosen_tokens.reshape(selected_count, 1, head_total_count, head_feature_width)
        * selection_mask[None, :, :, None]
    )
    return dilation_spread.reshape(selected_count * FAR_DILATION, feature_channel_width)


def to_heads(array):
    return array.reshape(array.shape[0], ATTENTION_HEADS, -1).transpose(1, 0, 2)


def from_heads(array):
    return array.transpose(1, 0, 2).reshape(array.shape[1], -1)


def head_pass(operands, positions, length):
    query_rows, key_rows, value_rows, distant_keys, far_values, context_gradient, start_offset = (
        operands
    )
    total_row_count, head_feature_width = query_rows.shape
    selected_count = total_row_count // FAR_DILATION
    segments = total_row_count // SEGMENT
    score_scale_factor = 1.0 / math.sqrt(head_feature_width)
    valid_token_mask = positions < length
    column_active = jnp.arange(FAR_DILATION, dtype=jnp.int32) == start_offset
    distant_positions = (
        jnp.arange(distant_keys.shape[0], dtype=jnp.int32) * FAR_DILATION + start_offset
    )
    query_segment = query_rows.reshape(segments, SEGMENT, head_feature_width)
    key_segment = key_rows.reshape(segments, SEGMENT, head_feature_width)
    value_segment = value_rows.reshape(segments, SEGMENT, head_feature_width)
    segment_gradient = context_gradient.reshape(segments, SEGMENT, head_feature_width)
    local_scores = (
        jnp.einsum("mhr,mtr->mht", query_segment, key_segment, preferred_element_type=jnp.float32)
        * score_scale_factor
    )
    local_scores = jnp.where(
        valid_token_mask.reshape(segments, SEGMENT)[:, None, :], local_scores, NEGATIVE
    )
    query_selected = lax.dynamic_index_in_dim(
        query_rows.reshape(selected_count, FAR_DILATION, head_feature_width),
        start_offset,
        1,
        keepdims=False,
    )
    selected_gradient = lax.dynamic_index_in_dim(
        context_gradient.reshape(selected_count, FAR_DILATION, head_feature_width),
        start_offset,
        1,
        keepdims=False,
    )
    far_scores = (
        jnp.einsum("qd,kd->qk", query_selected, distant_keys, preferred_element_type=jnp.float32)
        * score_scale_factor
    )
    far_scores = jnp.where((distant_positions < length)[None, :], far_scores, NEGATIVE)
    local_maximum = jnp.max(local_scores, axis=-1).reshape(selected_count, FAR_DILATION)
    far_peak = jnp.max(far_scores, axis=-1)
    pick_peak = jnp.maximum(
        lax.dynamic_index_in_dim(local_maximum, start_offset, 1, keepdims=False), far_peak
    )
    row_peak = jnp.where(column_active[None, :], pick_peak[:, None], local_maximum)
    local_exponent = jnp.exp(local_scores - row_peak.reshape(segments, SEGMENT)[:, :, None])
    distant_exponent = jnp.exp(far_scores - pick_peak[:, None])
    softmax_denominator = jnp.sum(local_exponent, axis=-1).reshape(
        selected_count, FAR_DILATION
    ) + jnp.where(column_active[None, :], jnp.sum(distant_exponent, axis=-1)[:, None], 0.0)
    row_weight_factor = (
        valid_token_mask.astype(jnp.float32).reshape(selected_count, FAR_DILATION)
        / softmax_denominator
    )
    pick_weight = lax.dynamic_index_in_dim(row_weight_factor, start_offset, 1, keepdims=False)
    near_prob = local_exponent * row_weight_factor.reshape(segments, SEGMENT)[:, :, None]
    far_prob = distant_exponent * pick_weight[:, None]
    local_rounded = near_prob.astype(jnp.bfloat16)
    far_round = far_prob.astype(jnp.bfloat16)
    local_output = jnp.einsum(
        "wun,wnj->wuj", local_rounded, value_segment, preferred_element_type=jnp.float32
    ).reshape(selected_count, FAR_DILATION, head_feature_width)
    far_out = jnp.einsum("qk,kd->qd", far_round, far_values, preferred_element_type=jnp.float32)
    context = (
        (local_output + jnp.where(column_active[None, :, None], far_out[:, None, :], 0.0))
        .reshape(total_row_count, head_feature_width)
        .astype(jnp.bfloat16)
    )
    row_delta_terms = jnp.sum(
        context.astype(jnp.float32) * context_gradient.astype(jnp.float32), axis=-1
    )
    selected_delta = lax.dynamic_index_in_dim(
        row_delta_terms.reshape(selected_count, FAR_DILATION), start_offset, 1, keepdims=False
    )
    local_probability_gradient = jnp.einsum(
        "mhr,mtr->mht", segment_gradient, value_segment, preferred_element_type=jnp.float32
    )
    local_score_gradient = (
        near_prob
        * (local_probability_gradient - row_delta_terms.reshape(segments, SEGMENT)[:, :, None])
        * score_scale_factor
    ).astype(jnp.bfloat16)
    far_dp = jnp.einsum(
        "qd,kd->qk", selected_gradient, far_values, preferred_element_type=jnp.float32
    )
    far_ds = (far_prob * (far_dp - selected_delta[:, None]) * score_scale_factor).astype(
        jnp.bfloat16
    )
    local_query_gradient = jnp.einsum(
        "wun,wnj->wuj", local_score_gradient, key_segment, preferred_element_type=jnp.float32
    ).reshape(selected_count, FAR_DILATION, head_feature_width)
    far_dq = jnp.einsum("qk,kd->qd", far_ds, distant_keys, preferred_element_type=jnp.float32)
    d_queries = (
        (local_query_gradient + jnp.where(column_active[None, :, None], far_dq[:, None, :], 0.0))
        .reshape(total_row_count, head_feature_width)
        .astype(jnp.bfloat16)
    )
    keys_gradient = jnp.einsum(
        "pjz,pjn->pzn", local_score_gradient, query_segment, preferred_element_type=jnp.float32
    ).reshape(total_row_count, head_feature_width)
    values_gradient = jnp.einsum(
        "pjz,pjn->pzn", local_rounded, segment_gradient, preferred_element_type=jnp.float32
    ).reshape(total_row_count, head_feature_width)
    d_far_keys = jnp.einsum("qk,qd->kd", far_ds, query_selected, preferred_element_type=jnp.float32)
    d_far_values = jnp.einsum(
        "qk,qd->kd", far_round, selected_gradient, preferred_element_type=jnp.float32
    )
    return (context, d_queries, keys_gradient, values_gradient, d_far_keys, d_far_values)


def local(patches, w_query, w_key, w_value, w_out, lengths, cotangent):
    tokens = patches[0]
    cot_rows = cotangent[0]
    total_row_count = tokens.shape[0]
    length = lengths[0]
    positions = lax.axis_index("seq") * total_row_count + jnp.arange(
        total_row_count, dtype=jnp.int32
    )
    query_rows = jnp.dot(tokens, w_query, preferred_element_type=jnp.float32).astype(jnp.bfloat16)
    key_rows = jnp.dot(tokens, w_key, preferred_element_type=jnp.float32).astype(jnp.bfloat16)
    value_rows = jnp.dot(tokens, w_value, preferred_element_type=jnp.float32).astype(jnp.bfloat16)
    chosen_tokens = pick_rows(jnp.stack([key_rows, value_rows]), ATTENTION_HEADS)
    far_pair = lax.all_gather(chosen_tokens, "seq", axis=1, tiled=True)
    context_gradient = jnp.dot(cot_rows, w_out.T, preferred_element_type=jnp.float32).astype(
        jnp.bfloat16
    )
    start_offsets = jnp.arange(ATTENTION_HEADS, dtype=jnp.int32) % FAR_DILATION
    operands = (
        to_heads(query_rows),
        to_heads(key_rows),
        to_heads(value_rows),
        to_heads(far_pair[0]),
        to_heads(far_pair[1]),
        to_heads(context_gradient),
        start_offsets,
    )
    results = lax.map(lambda segment_member: head_pass(segment_member, positions, length), operands)
    context, d_queries, keys_gradient, values_gradient = (
        results[0],
        results[1],
        results[2],
        results[3],
    )
    far_grads = jnp.stack([from_heads(results[4]), from_heads(results[5])])
    own_grads = lax.psum_scatter(far_grads, "seq", scatter_dimension=1, tiled=True)
    context_all = from_heads(context)
    dq_all = from_heads(d_queries)
    dk_all = (from_heads(keys_gradient) + place_rows(own_grads[0], ATTENTION_HEADS)).astype(
        jnp.bfloat16
    )
    dv_all = (from_heads(values_gradient) + place_rows(own_grads[1], ATTENTION_HEADS)).astype(
        jnp.bfloat16
    )
    attended = jnp.dot(context_all, w_out, preferred_element_type=jnp.float32).astype(jnp.bfloat16)
    grad_rows = (
        jnp.dot(dq_all, w_query.T, preferred_element_type=jnp.float32)
        + jnp.dot(dk_all, w_key.T, preferred_element_type=jnp.float32)
        + jnp.dot(dv_all, w_value.T, preferred_element_type=jnp.float32)
    ).astype(jnp.bfloat16)
    partials = (
        jnp.einsum("rd,re->de", tokens, dq_all, preferred_element_type=jnp.float32),
        jnp.einsum("rd,re->de", tokens, dk_all, preferred_element_type=jnp.float32),
        jnp.einsum("rd,re->de", tokens, dv_all, preferred_element_type=jnp.float32),
        jnp.einsum("rd,re->de", context_all, cot_rows, preferred_element_type=jnp.float32),
    )
    totals = lax.psum((partials[0], partials[1], partials[2], partials[3]), ("seq", "slide"))
    grads = tuple((segment_member.astype(jnp.bfloat16) for segment_member in totals))
    return (attended[None], grad_rows[None], grads[0], grads[1], grads[2], grads[3])


def solution(mesh):
    placed = (P("slide", "seq", None), P(), P(), P(), P(), P("slide"), P("slide", "seq", None))
    return jax.shard_map(
        local,
        mesh=mesh,
        in_specs=placed,
        out_specs=(P("slide", "seq", None), P("slide", "seq", None), P(), P(), P(), P()),
        check_vma=False,
    )
```

profile of v0, /device:TPU:1, one launch (start us, length us, event | category | flops | bytes accessed | tf_op | source)
XLA Modules:
  0.0 1068.9 jit_solution(7181562807502427691)
XLA Ops:
  28.9 5.9 stack.16
  34.8 5.3 copy.612
  54.1 34.2 %all-gather.2.cloned.1.call-done = bf16[2,1024,768]{1,2,0:T(8,128)(2,1)} async-done(((bf16[2,256,768]{1,2,0:T(8,128)(2,1)}), bf16[2,1024,768]{1,2,0:T(8,128)(2,1)}) %all-gather.2.cloned.1.call-update) | async-done | bytes 3145744 | tf_op jit(solution)/shard_map/all_gather | solution.py:178
  92.2 678.5 %while.21 = (s32[]{:T(128)}, bf16[12,1024,64]{1,2,0:T(8,128)(2,1)}, bf16[12,1024,64]{1,2,0:T(8,128)(2,1)}, f32[12,1024,64]{1,2,0:T(8,128)}, f32[12,1024,64]{1,2,...) while((s32[]{:T(128)}, bf16[12,1024,64]{1,2,0:T(8,128)(2,1)}, ...), condition=%wide.region_6.7_spmd.clone, body=%wide.region_0.6_spmd.clone.sunk | while | flops 1031942656 | bytes 82001000 | solution.py:192
  128.8 5.1 multiply_convert_fusion.8
  185.2 5.1 multiply_convert_fusion.8
  241.7 5.1 multiply_convert_fusion.8
  298.2 5.1 multiply_convert_fusion.8
  354.6 5.1 multiply_convert_fusion.8
  411.1 5.1 multiply_convert_fusion.8
  467.6 5.1 multiply_convert_fusion.8
  524.1 5.1 multiply_convert_fusion.8
  770.7 6.6 pad_maximum_fusion
  790.7 52.6 %reduce-scatter.2.cloned.1.call-done = f32[2,256,768]{1,2,0:T(8,128)} async-done(((f32[2,1024,768]{1,2,0:T(8,128)}), f32[2,256,768]{1,2,0:T(8,128)}) %reduce-scatter.2.cloned.1.call-update) | async-done | bytes 1572880 | tf_op jit(solution)/shard_map/reduce_scatter | solution.py:200
  851.4 6.2 copy.626
  860.3 6.8 broadcast_multiply_fusion.1
  870.8 6.1 copy.627
  876.9 6.4 fusion.68
  888.9 114.4 %all-reduce.2 = (bf16[768,768]{0,1:T(8,128)(2,1)}, bf16[768,768]{0,1:T(8,128)(2,1)}, bf16[768,768]{0,1:T(8,128)(2,1)S(1)}, bf16[768,768]{1,0:T(8,128)(2,1)}) all-reduce(f32[768,768]{0,1:T(8,128)} %convolution_bitcast_fusion.6, f32[768,768]{0,1:T(8,128)} %convolution_bitcast_fusion.5, ...), channel_id=1, replica_groups=mesh['seq'=4,'slide'=32] {'seq','slide'}, use_global_device_ids=true, to_apply=%region_8.9 | all-reduce | flops 2359296 | bytes 14155776 | tf_op jit(solution)/shard_map/psum | solution.py:221
  1009.5 9.8 copy.619
  1019.3 7.3 mul.119
  1030.1 9.9 copy.622
  1040.0 7.5 mul.123
  1051.0 5.8 fusion.66
  (1044 shorter events, 700.9 us)
Async XLA Ops:
  7.2 81.2 %all-gather.2.cloned.1.call-start = ((), (), s32[]{:S(2)}) async-start(), calls=%async_computation.1 | async-start | bytes 3932160 | tf_op jit(solution)/shard_map/all_gather | solution.py:178
  42.6 800.8 %reduce-scatter.2.cloned.1.call-start = ((), (), s32[]{:S(2)}) async-start(), calls=%async_computation.2 | async-start | bytes 7864320 | tf_op jit(solution)/shard_map/reduce_scatter | solution.py:200
  104.9 10.7 %copy-start.16 = (pred[4]{0:T(512)(128)(4,1)}, pred[4]{0:T(512)(128)(4,1)S(1)}, u32[]{:S(2)}) copy-start(pred[4]{0:T(512)(128)(4,1)S(1)} %iota_compare_fusion.3) | copy-start | bytes 16 | tf_op jit(solution)/shard_map/while
  133.9 4.2 copy-start.17
  161.4 10.7 %copy-start.16 = (pred[4]{0:T(512)(128)(4,1)}, pred[4]{0:T(512)(128)(4,1)S(1)}, u32[]{:S(2)}) copy-start(pred[4]{0:T(512)(128)(4,1)S(1)} %iota_compare_fusion.3) | copy-start | bytes 16 | tf_op jit(solution)/shard_map/while
  190.3 4.2 copy-start.17
  217.9 10.7 %copy-start.16 = (pred[4]{0:T(512)(128)(4,1)}, pred[4]{0:T(512)(128)(4,1)S(1)}, u32[]{:S(2)}) copy-start(pred[4]{0:T(512)(128)(4,1)S(1)} %iota_compare_fusion.3) | copy-start | bytes 16 | tf_op jit(solution)/shard_map/while
  246.8 4.2 copy-start.17
  274.4 10.7 %copy-start.16 = (pred[4]{0:T(512)(128)(4,1)}, pred[4]{0:T(512)(128)(4,1)S(1)}, u32[]{:S(2)}) copy-start(pred[4]{0:T(512)(128)(4,1)S(1)} %iota_compare_fusion.3) | copy-start | bytes 16 | tf_op jit(solution)/shard_map/while
  330.8 10.7 %copy-start.16 = (pred[4]{0:T(512)(128)(4,1)}, pred[4]{0:T(512)(128)(4,1)S(1)}, u32[]{:S(2)}) copy-start(pred[4]{0:T(512)(128)(4,1)S(1)} %iota_compare_fusion.3) | copy-start | bytes 16 | tf_op jit(solution)/shard_map/while
  387.3 10.7 %copy-start.16 = (pred[4]{0:T(512)(128)(4,1)}, pred[4]{0:T(512)(128)(4,1)S(1)}, u32[]{:S(2)}) copy-start(pred[4]{0:T(512)(128)(4,1)S(1)} %iota_compare_fusion.3) | copy-start | bytes 16 | tf_op jit(solution)/shard_map/while
  416.3 4.2 copy-start.17
  443.8 10.7 %copy-start.16 = (pred[4]{0:T(512)(128)(4,1)}, pred[4]{0:T(512)(128)(4,1)S(1)}, u32[]{:S(2)}) copy-start(pred[4]{0:T(512)(128)(4,1)S(1)} %iota_compare_fusion.3) | copy-start | bytes 16 | tf_op jit(solution)/shard_map/while
  472.7 4.2 copy-start.17
  500.3 10.7 %copy-start.16 = (pred[4]{0:T(512)(128)(4,1)}, pred[4]{0:T(512)(128)(4,1)S(1)}, u32[]{:S(2)}) copy-start(pred[4]{0:T(512)(128)(4,1)S(1)} %iota_compare_fusion.3) | copy-start | bytes 16 | tf_op jit(solution)/shard_map/while
  529.2 4.2 copy-start.17
  556.8 10.7 %copy-start.16 = (pred[4]{0:T(512)(128)(4,1)}, pred[4]{0:T(512)(128)(4,1)S(1)}, u32[]{:S(2)}) copy-start(pred[4]{0:T(512)(128)(4,1)S(1)} %iota_compare_fusion.3) | copy-start | bytes 16 | tf_op jit(solution)/shard_map/while
  613.4 10.7 %copy-start.16 = (pred[4]{0:T(512)(128)(4,1)}, pred[4]{0:T(512)(128)(4,1)S(1)}, u32[]{:S(2)}) copy-start(pred[4]{0:T(512)(128)(4,1)S(1)} %iota_compare_fusion.3) | copy-start | bytes 16 | tf_op jit(solution)/shard_map/while
  669.9 10.7 %copy-start.16 = (pred[4]{0:T(512)(128)(4,1)}, pred[4]{0:T(512)(128)(4,1)S(1)}, u32[]{:S(2)}) copy-start(pred[4]{0:T(512)(128)(4,1)S(1)} %iota_compare_fusion.3) | copy-start | bytes 16 | tf_op jit(solution)/shard_map/while
  726.4 10.7 %copy-start.16 = (pred[4]{0:T(512)(128)(4,1)}, pred[4]{0:T(512)(128)(4,1)S(1)}, u32[]{:S(2)}) copy-start(pred[4]{0:T(512)(128)(4,1)S(1)} %iota_compare_fusion.3) | copy-start | bytes 16 | tf_op jit(solution)/shard_map/while
  777.8 4.4 copy-start.20
  777.8 4.4 copy-start.21
  860.3 6.8 copy-start.6
  1051.0 5.9 copy-start.25
  (158 other events, 385.0 us)
Sparse Core Ops, SparseCore 0:
  42.7 45.5 all-gather.1
  777.5 65.8 reduce-scatter.1
where the time goes:
time: 1080 us; the launch traced here: 1070 us
  matrix products  359 us (33%)
  local copies, waits for them, and re-layouts  305 us (28%)
  other arithmetic  161 us (15%)
  blocking collectives  114 us (11%)
  waiting for transfers between devices  86.9 us (8%)
  loops' own time  27.8 us (3%)
  between operations  14.5 us (1%)
    psum x1, blocking collectives, local(): lax.psum((partials[0], partials[1], partials[2], partials[3]), ('seq', 's...  114 us
    mul x14, local copies, waits for them, and re-layouts, place_rows(): chosen_tokens.reshape(selected_count, 1, head_total_count, head_feature_w...  65.9 us
    dot_general x12, matrix products, head_pass(): jnp.einsum('mhr,mtr->mht', segment_gradient, value_segment, preferred_ele...  61.3 us
    reduce_scatter x1, waiting for transfers between devices, local(): lax.psum_scatter(far_grads, 'seq', scatter_dimension=1, tiled=True)  52.6 us
    dot_general x12, local copies, waits for them, and re-layouts, head_pass(): jnp.einsum('wun,wnj->wuj', local_score_gradient, key_segment, preferred_e...  49.9 us
    dot_general x12, local copies, waits for them, and re-layouts, head_pass(): jnp.einsum('wun,wnj->wuj', local_rounded, value_segment, preferred_elemen...  49.3 us
    dot_general x12, matrix products, head_pass(): jnp.einsum('mhr,mtr->mht', query_segment, key_segment, preferred_element_...  43.4 us
    reduce_sum x12, other arithmetic, head_pass(): jnp.sum(local_exponent, axis=-1).reshape(selected_count, FAR_DILATION)  39.9 us
  transfers between devices with their start and end apart: 2, of which 2 were waited for; matrix products, arithmetic and copies ran while one was open for 2% of the time, Pallas kernels for 0%

commit v1 on v0

v1 whole, which is shorter than its diff:
```python
import math

import jax
import jax.numpy as jnp
from jax import lax
from jax.experimental import pallas as pl
from jax.experimental.pallas import tpu as pltpu
from jax.sharding import PartitionSpec as P

BF, F32 = jnp.bfloat16, jnp.float32
NEGATIVE = -1e30
ROWS, D, HEAD, PAIRS = 1024, 768, 64, 6
FAR = 256
LN2 = math.log(2.0)
QUERY_SCALE = 1.0 / (math.sqrt(HEAD) * LN2)
VMEM_LIMIT = 56 << 20


def nn(a, b):
    return lax.dot_general(a, b, (((1,), (0,)), ((), ())), preferred_element_type=F32)


def nt(a, b):
    return lax.dot_general(a, b, (((1,), (1,)), ((), ())), preferred_element_type=F32)


def selection(transposed):
    a = lax.broadcasted_iota(jnp.int32, (512, 512), 1 if transposed else 0)
    b = lax.broadcasted_iota(jnp.int32, (512, 512), 0 if transposed else 1)
    return jnp.where(4 * (a & 127) + (a >> 7) == b, 1.0, 0.0).astype(BF)


def project_kernel(x, cot, wq, wk, wv, wo, xp, cp, q, k, v, do, far):
    pick = selection(False)
    rows = nn(pick, x[...]).astype(BF)
    cots = nn(pick, cot[...]).astype(BF)
    qs = (nn(rows, wq[...]) * QUERY_SCALE).astype(BF)
    ks = nn(rows, wk[...]).astype(BF)
    vs = nn(rows, wv[...]).astype(BF)
    ds = nt(cots, wo[...]).astype(BF)
    for ref, value in ((xp, rows), (cp, cots), (q, qs), (k, ks), (v, vs), (do, ds)):
        for c in range(4):
            ref[c] = value[c * 128 : c * 128 + 128]
    left = lax.broadcasted_iota(jnp.int32, (128, 128), 1) < HEAD
    for n, value in ((0, ks), (1, vs)):
        for t in range(PAIRS):
            c = 2 * (t % 2)
            at = slice(t * 128, t * 128 + 128)
            far[n, :, at] = jnp.where(
                left, value[c * 128 : c * 128 + 128, at], value[c * 128 + 128 : c * 128 + 256, at]
            )


def attend_kernel(info, q, k, v, do, far, ctxT, dqT, dkT, dvT, dfar, e_scr, ds_scr, t_scr):
    pair = pl.program_id(0)
    length, base = info[0], info[1]
    zero, one = jnp.zeros((), BF), jnp.ones((), BF)
    qT, doT, kT, vT = q[...].T, do[...].T, k[...].T, v[...].T
    kf = far[:, 0].reshape(ROWS, 128)
    vf = far[:, 1].reshape(ROWS, 128)
    kfT, vfT = kf.T, vf.T
    lane = lax.broadcasted_iota(jnp.int32, (ROWS, 128), 1)
    row = lax.broadcasted_iota(jnp.int32, (ROWS, 128), 0)
    sub = lax.broadcasted_iota(jnp.int32, (128, ROWS), 0)
    near_bias = jnp.where(4 * (row & 255) + (row >> 8) + base < length, 0.0, NEGATIVE).astype(BF)
    rq = lax.broadcasted_iota(jnp.int32, (1, ROWS), 1)
    real = jnp.where(4 * (rq & 255) + (rq >> 8) + base < length, 1.0, 0.0)
    tail = jnp.where(lax.broadcasted_iota(jnp.int32, (16, ROWS), 0) == 0, 1.0, 0.0).astype(BF)
    for a in range(2):
        o = HEAD * (1 - a)
        c = 2 * (pair & 1) + a
        mine = (lane < HEAD) if a == 0 else (lane >= HEAD)
        mine_t = (sub < HEAD) if a == 0 else (sub >= HEAD)
        sl = slice(HEAD * a, HEAD * a + HEAD)
        far_bias = jnp.where(4 * row + c < length, 0.0, NEGATIVE).astype(BF)
        ones2 = jnp.where((lane == o) | (lane == o + 1), one, zero)
        ka = jnp.where(mine, k[...], jnp.where(lane == o, near_bias, zero))
        kfa = jnp.where(mine, kf, jnp.where(lane == o, far_bias, zero))
        va = jnp.where(mine, v[...], ones2)
        vfa = jnp.where(mine, vf, ones2)
        t_scr[1] = jnp.where(mine_t, qT, jnp.where(sub == o, one, zero))
        t_scr[2] = doT
        t_scr[3, 0:1, :] = real.astype(BF)
        vta = jnp.concatenate([vT[sl], tail], axis=0)
        vfta = jnp.concatenate([vfT[sl], tail], axis=0)
        kta, kfta = kT[sl], kfT[sl]
        for b in range(4):
            at = pl.ds(pl.multiple_of(((c + b) & 3) * 256, 256), 256)
            qb = t_scr[1, :, at]
            s = nn(ka, qb)
            peak = jnp.max(s, axis=0, keepdims=True)
            if b == 0:
                sf = nn(kfa, qb)
                peak = jnp.maximum(peak, jnp.max(sf, axis=0, keepdims=True))
            e = jnp.exp2(s - peak).astype(BF)
            out = nn(vta, e)
            if b == 0:
                ef = jnp.exp2(sf - peak).astype(BF)
                out = out + nn(vfta, ef)
            weight = t_scr[3, 0:1, at].astype(F32) / out[HEAD : HEAD + 1]
            cx = (out[:HEAD] * weight).astype(BF)
            ctxT[sl, at] = cx
            dob = t_scr[2, sl, at].astype(F32)
            shift = -weight * jnp.sum(cx.astype(F32) * dob, axis=0, keepdims=True)
            high = shift.astype(BF)
            low = (shift - high.astype(F32)).astype(BF)
            dw = (dob * weight).astype(BF)
            sub2 = lax.broadcasted_iota(jnp.int32, (HEAD, 256), 0)
            extra = jnp.where(sub2 == 0, high, jnp.where(sub2 == 1, low, zero))
            dwa = jnp.concatenate([dw, extra] if a == 0 else [extra, dw], axis=0)
            ds = e * nn(va, dwa).astype(BF)
            dq = nn(kta, ds)
            if b == 0:
                dsf = ef * nn(vfa, dwa).astype(BF)
                dq = dq + nn(kfta, dsf)
                dfk = (nt(qb[sl], dsf) * LN2).astype(BF)
                dfv = nt(dw, ef).astype(BF)
                for j in range(4):
                    dfar[j, 0, sl, :] = dfk[:, j * FAR : j * FAR + FAR]
                    dfar[j, 1, sl, :] = dfv[:, j * FAR : j * FAR + FAR]
            dqT[sl, at] = (dq * 0.125).astype(BF)
            e_scr[:, at] = e
            ds_scr[:, at] = ds
            t_scr[0, sl, at] = dw
        dkT[sl, :] = nt(t_scr[1, sl, :], ds_scr[...]) * LN2
        dvT[sl, :] = nt(t_scr[0, sl, :], e_scr[...])


def finish_kernel(ctxT, dqT, dkT, dvT, own, xp, cp, wq, wk, wv, wo, att, gx, grads, dkb, dvb):
    for h in range(2 * PAIRS):
        sl = slice(h * HEAD, h * HEAD + HEAD)
        c = h % 4
        for n, (src, dst) in enumerate(((dkT, dkb), (dvT, dvb))):
            for b in range(4):
                at = slice(b * FAR, b * FAR + FAR)
                value = src[sl, at]
                if b == c:
                    value = value + own[n, sl, :].astype(F32)
                dst[sl, at] = value.astype(BF)
    grads[3] = nn(ctxT[...], cp[...])
    grads[0] = nn(dqT[...], xp[...])
    grads[1] = nn(dkb[...], xp[...])
    grads[2] = nn(dvb[...], xp[...])
    place = selection(True)
    woT = wo[...].T
    for j in range(2):
        def part(ref):
            return jnp.concatenate(
                [ref[:, c * FAR + j * 128 : c * FAR + j * 128 + 128] for c in range(4)], axis=1
            )

        outT = nn(woT, part(ctxT)).astype(BF)
        att[j * 512 : j * 512 + 512, :] = nt(place, outT).astype(BF)
        gT = nn(wq[...], part(dqT)) + nn(wk[...], part(dkb)) + nn(wv[...], part(dvb))
        gx[j * 512 : j * 512 + 512, :] = nt(place, gT.astype(BF)).astype(BF)


def project(tokens, cots, wq, wk, wv, wo):
    rows = pl.BlockSpec((512, D), lambda j: (j, 0))
    whole = pl.BlockSpec((D, D), lambda j: (0, 0))
    out = pl.BlockSpec((4, 128, D), lambda j: (0, j, 0))
    shape = jax.ShapeDtypeStruct((4, FAR, D), BF)
    return pl.pallas_call(
        project_kernel,
        grid=(2,),
        in_specs=[rows, rows, whole, whole, whole, whole],
        out_specs=[out] * 6 + [pl.BlockSpec((2, 128, D), lambda j: (0, j, 0))],
        out_shape=[shape] * 6 + [jax.ShapeDtypeStruct((2, FAR, D), BF)],
        compiler_params=pltpu.CompilerParams(vmem_limit_bytes=VMEM_LIMIT),
    )(tokens, cots, wq, wk, wv, wo)


def attend(info, q, k, v, do, far):
    col = pl.BlockSpec((ROWS, 128), lambda i: (0, i))
    row = pl.BlockSpec((128, ROWS), lambda i: (i, 0))
    return pl.pallas_call(
        attend_kernel,
        grid=(PAIRS,),
        in_specs=[
            pl.BlockSpec(memory_space=pltpu.SMEM),
            col,
            col,
            col,
            col,
            pl.BlockSpec((4, 2, FAR, 128), lambda i: (0, 0, 0, i)),
        ],
        out_specs=[row, row, row, row, pl.BlockSpec((4, 2, 128, FAR), lambda i: (0, 0, i, 0))],
        out_shape=[
            jax.ShapeDtypeStruct((D, ROWS), BF),
            jax.ShapeDtypeStruct((D, ROWS), BF),
            jax.ShapeDtypeStruct((D, ROWS), F32),
            jax.ShapeDtypeStruct((D, ROWS), F32),
            jax.ShapeDtypeStruct((4, 2, D, FAR), BF),
        ],
        scratch_shapes=[
            pltpu.VMEM((ROWS, ROWS), BF),
            pltpu.VMEM((ROWS, ROWS), BF),
            pltpu.VMEM((4, 128, ROWS), BF),
        ],
        compiler_params=pltpu.CompilerParams(vmem_limit_bytes=VMEM_LIMIT),
    )(info, q, k, v, do, far)


def finish(*operands):
    return pl.pallas_call(
        finish_kernel,
        out_shape=[
            jax.ShapeDtypeStruct((ROWS, D), BF),
            jax.ShapeDtypeStruct((ROWS, D), BF),
            jax.ShapeDtypeStruct((4, D, D), F32),
        ],
        scratch_shapes=[pltpu.VMEM((D, ROWS), BF), pltpu.VMEM((D, ROWS), BF)],
        compiler_params=pltpu.CompilerParams(vmem_limit_bytes=VMEM_LIMIT),
    )(*operands)


def local(patches, wq, wk, wv, wo, lengths, cotangent):
    base = lax.axis_index("seq").astype(jnp.int32) * ROWS
    info = jnp.stack([lengths[0], base])
    xp, cp, q, k, v, do, far = project(patches[0], cotangent[0], wq, wk, wv, wo)
    flat = lambda t: t.reshape(ROWS, D)
    far_all = lax.all_gather(far, "seq", axis=0)
    ctxT, dqT, dkT, dvT, dfar = attend(info, flat(q), flat(k), flat(v), flat(do), far_all)
    own = lax.psum_scatter(dfar, "seq", scatter_dimension=0, tiled=False)
    att, gx, grads = finish(ctxT, dqT, dkT, dvT, own, flat(xp), flat(cp), wq, wk, wv, wo)
    totals = lax.psum(grads, ("seq", "slide")).astype(BF)
    return (att[None], gx[None], totals[0].T, totals[1].T, totals[2].T, totals[3])


def solution(mesh):
    split = P("slide", "seq", None)
    return jax.shard_map(
        local,
        mesh=mesh,
        in_specs=(split, P(), P(), P(), P(), P("slide"), split),
        out_specs=(split, split, P(), P(), P(), P()),
        check_vma=False,
    )
```

time: 1080 us -> 340 us (0.31)
  matrix products: 359 us -> 0 us
  local copies, waits for them, and re-layouts: 305 us -> 7.98 us
  other arithmetic: 161 us -> 0.59 us
  Pallas kernels: 0 us -> 122 us
  loops' own time: 27.8 us -> 0 us
    dot_general x156 -> x0, matrix products: 359 us -> none  [the longest x12 61.3 us: head_pass(): jnp.einsum('mhr,mtr->mht', segment_gradient, value_segment, preferred_ele...]
    pallas_call x0 -> x3, Pallas kernels: none -> 122 us  [the longest x1 88.1 us: attend(): pl.pallas_call(attend_kernel, grid=(PAIRS,), in_specs=[pl.BlockSpec(memor...]
    dot_general x24 -> x0, local copies, waits for them, and re-layouts: 99.1 us -> none  [the longest x12 49.9 us: head_pass(): jnp.einsum('wun,wnj->wuj', local_score_gradient, key_segment, preferred_e...]
    mul x14 -> x0, local copies, waits for them, and re-layouts: 65.9 us -> none  [place_rows(): chosen_tokens.reshape(selected_count, 1, head_total_count, head_feature_w...]
    convert_element_type x39 -> x0, other arithmetic: 50.5 us -> none  [the longest x12 27.7 us: head_pass(): local_rounded = near_prob.astype(jnp.bfloat16)]
    dynamic_slice x108 -> x0, local copies, waits for them, and re-layouts: 49.8 us -> none  [the longest x36 30.3 us: local(): lax.map(lambda segment_member: head_pass(segment_member, positions, lengt...]
    reduce_sum x24 -> x0, other arithmetic: 43.6 us -> none  [the longest x12 39.9 us: head_pass(): jnp.sum(local_exponent, axis=-1).reshape(selected_count, FAR_DILATION)]
    another operation x1 -> x0, loops' own time: 27.8 us -> none  [local(): lax.map(lambda segment_member: head_pass(segment_member, positions, lengt...]
  transfers between devices with their start and end apart: 2 -> 2, of which waited for: 2 -> 2; matrix products, arithmetic and copies ran while one was open for 2% -> 0% of each run, Pallas kernels for 0% -> 0%
where the time goes in v1:
time: 340 us; the launch traced here: 339 us
  Pallas kernels  122 us (36%)
  blocking collectives  113 us (33%)
  waiting for transfers between devices  80.1 us (24%)
  between operations  14.7 us (4%)
  local copies, waits for them, and re-layouts  7.98 us (2%)
    psum x1, blocking collectives, local(): totals = lax.psum(grads, ('seq', 'slide')).astype(BF)  113 us
    pallas_call x1, Pallas kernels, attend(): pl.pallas_call(attend_kernel, grid=(PAIRS,), in_specs=[pl.BlockSpec(memor...  88.1 us
    all_gather x1, waiting for transfers between devices, local(): far_all = lax.all_gather(far, 'seq', axis=0)  41.5 us
    reduce_scatter x1, waiting for transfers between devices, local(): own = lax.psum_scatter(dfar, 'seq', scatter_dimension=0, tiled=False)  38.6 us
    pallas_call x1, Pallas kernels, finish(): pl.pallas_call(finish_kernel, out_shape=[jax.ShapeDtypeStruct((ROWS, D),...  22 us
    pallas_call x1, Pallas kernels, project(): pl.pallas_call(project_kernel, grid=(2,), in_specs=[rows, rows, whole, wh...  12.1 us
  transfers between devices with their start and end apart: 2, of which 2 were waited for; matrix products, arithmetic and copies ran while one was open for 0% of the time, Pallas kernels for 0%

profile of v1, /device:TPU:1, one launch (start us, length us, event | category | flops | bytes accessed | tf_op | source)
XLA Modules:
  0.0 339.3 jit_solution(14496858597283956562)
XLA Ops:
  7.2 0.0 all-gather.3.cloned.1.call-start
  7.2 12.1 %shard_map.118 = (bf16[4,256,768]{2,1,0:T(8,128)(2,1)}, bf16[4,256,768]{2,1,0:T(8,128)(2,1)}, bf16[4,256,768]{2,1,0:T(8,128)(2,1)}, bf16[4,256,768]{2,1,0:T(8,12...) custom-call(bf16[1024,768]{1,0:T(8,128)(2,1)} %bitcast.34, ...), custom_call_target="tpu_custom_call" | custom-call | tf_op jit(solution)/shard_map/pallas_call | solution.py:163
  19.3 0.0 all-gather.3.cloned.1.call-update
  19.3 0.2 reduce-scatter.2.cloned.1.call-start
  20.2 0.6 pad_add_fusion.info
  20.8 41.5 %all-gather.3.cloned.1.call-done = bf16[8,256,768]{2,1,0:T(8,128)(2,1)} async-done(((bf16[2,256,768]{2,1,0:T(8,128)(2,1)}), bf16[8,256,768]{2,1,0:T(8,128)(2,1)}) %all-gather.3.cloned.1.call-update) | async-done | bytes 3145744 | tf_op jit(solution)/shard_map/all_gather | solution.py:222
  62.3 88.1 %shard_map.119 = (bf16[768,1024]{1,0:T(8,128)(2,1)}, bf16[768,1024]{1,0:T(8,128)(2,1)}, f32[768,1024]{1,0:T(8,128)}, f32[768,1024]{1,0:T(8,128)}, bf16[4,2,768,256]{3,2,1,0:T(8,128)(2,1)}) custom-call(s32[2]{0:T(128)} %pad_add_fusion.info, bf16[1024,768]{1,0:T(8,128)(2,1)} %bitcast.30, bf16[1024,768]{1,0:T(8,128)(2,1)} %bitcast.31, ...), custom_call_target="tpu_custom_call" | custom-call | tf_op jit(solution)/shard_map/pallas_call | solution.py:176
  150.4 0.0 reduce-scatter.2.cloned.1.call-update
  150.4 38.6 %reduce-scatter.2.cloned.1.call-done = bf16[1,2,768,256]{3,2,1,0:T(8,128)(2,1)} async-done(((bf16[4,2,768,256]{3,2,1,0:T(8,128)(2,1)}), bf16[1,2,768,256]{3,2,1,0:T(8,128)(2,1)}) %reduce-scatter.2.cloned.1.call-update) | async-done | bytes 786448 | tf_op jit(solution)/shard_map/reduce_scatter | solution.py:224
  189.0 22.0 %shard_map.120 = (bf16[1024,768]{1,0:T(8,128)(2,1)}, bf16[1024,768]{1,0:T(8,128)(2,1)}, f32[4,768,768]{2,1,0:T(8,128)}) custom-call(bf16[768,1024]{1,0:T(8,128)(2,1)} %get-tuple-element.26.ctxT, bf16[768,1024]{1,0:T(8,128)(2,1)} %get-tuple-element.27.dqT, f32[768,1024]{1,0:T(8,128)} %get-tuple-element.28.dkT, f32[768,1024]{1,0:T(8,128)} %get-tuple-element.29.dvT, ...), custom_call_target="tpu_custom_call" | custom-call | tf_op jit(solution)/shard_map/pallas_call | solution.py:205
  211.0 113.5 %all-reduce.1 = bf16[4,768,768]{2,1,0:T(8,128)(2,1)} all-reduce(f32[4,768,768]{2,1,0:T(8,128)} %get-tuple-element.35), channel_id=1, replica_groups=mesh['seq'=4,'slide'=32] {'seq','slide'}, use_global_device_ids=true, to_apply=%region_1.0 | all-reduce | flops 2359296 | bytes 14155776 | tf_op jit(solution)/shard_map/psum | solution.py:226
  324.5 3.7 %slice_bitcast_fusion = (bf16[768,768]{1,0:T(8,128)(2,1)}, bf16[768,768]{0,1:T(8,128)(2,1)S(1)}, bf16[768,768]{0,1:T(8,128)(2,1)S(1)}, bf16[768,768]{0,1:T(8,128)(2,1)S(1)}) fusion(bf16[4,768,768]{2,1,0:T(8,128)(2,1)} %all-reduce.1), kind=kLoop, calls=%fused_computation | loop fusion | bytes 9437184 | tf_op jit(solution)/shard_map/squeeze | solution.py:227
  328.2 1.4 copy.18
  329.6 1.4 copy.17
  331.0 1.4 copy.16
Async XLA Ops:
  7.2 55.1 %all-gather.3.cloned.1.call-start = ((), (), s32[]{:S(2)}) async-start(), calls=%async_computation.2 | async-start | bytes 3932160 | tf_op jit(solution)/shard_map/all_gather | solution.py:222
  19.3 169.7 %reduce-scatter.2.cloned.1.call-start = ((), (), s32[]{:S(2)}) async-start(), calls=%async_computation.1 | async-start | bytes 3932160 | tf_op jit(solution)/shard_map/reduce_scatter | solution.py:224
Sparse Core Ops, SparseCore 0:
  19.5 42.7 all-gather.2
  150.5 38.4 reduce-scatter.1

commit v2 on v1

v2 whole, which is shorter than its diff:
```python
import math

import jax
import jax.numpy as jnp
from jax import lax
from jax.experimental import pallas as pl
from jax.experimental.pallas import tpu as pltpu
from jax.sharding import PartitionSpec as P

BF, F32 = jnp.bfloat16, jnp.float32
MESH = pl.DeviceIdType.MESH
NEGATIVE = -1e30
ROWS, D, HEAD, PAIRS = 1024, 768, 64, 6
FAR = 256
LN2 = math.log(2.0)
QUERY_SCALE = 1.0 / (math.sqrt(HEAD) * LN2)
VMEM_LIMIT = 60 << 20
PART, HALF, QUARTER, PIECE = 3072, 1536, 384, 96


def nn(a, b):
    return lax.dot_general(a, b, (((1,), (0,)), ((), ())), preferred_element_type=F32)


def nt(a, b):
    return lax.dot_general(a, b, (((1,), (1,)), ((), ())), preferred_element_type=F32)


def selection(transposed):
    a = lax.broadcasted_iota(jnp.int32, (512, 512), 1 if transposed else 0)
    b = lax.broadcasted_iota(jnp.int32, (512, 512), 0 if transposed else 1)
    return jnp.where(4 * (a & 127) + (a >> 7) == b, 1.0, 0.0).astype(BF)


def kernel(
    info, x_hbm, cot_hbm, wq_hbm, wk_hbm, wv_hbm, wo_hbm,
    att_hbm, gx_hbm, total,
    wq, wk, wv, wo, xpT, cp, q, k, v, do, far,
    ctxT, dqT, dkT, dvT, e_scr, ds_scr, t_scr, near,
    dfs, dfr, part, ar, bs, br, cs, xr, zr, fin,
    load_sem, far_s, far_r, df_s, df_r, a_s, a_r, b_s, b_r, x_s, x_r, z_s, z_r,
    gx_s, gx_r, gl_s, gy_s, gy_r, gc_s, gc_r, out_sem,
):
    y = lax.axis_index("seq").astype(jnp.int32)
    slide = lax.axis_index("slide").astype(jnp.int32)
    xi = lax.div(slide, 8)
    zi = lax.rem(lax.div(slide, 2), 4)
    core = lax.rem(slide, 2)
    length = info[0]
    base = y * ROWS

    def y_peer(n):
        return (lax.rem(y + n, 4), slide)

    def x_peer(n):
        return (y, slide + 8 * (lax.rem(xi + n, 4) - xi))

    def z_peer(n):
        return (y, slide + 2 * (lax.rem(zi + n, 4) - zi))

    sibling = (y, slide + 1 - 2 * core)

    loads = [
        pltpu.make_async_copy(src, dst, load_sem.at[n])
        for n, (src, dst) in enumerate(
            (
                (x_hbm, e_scr.at[:, 0:D]),
                (wk_hbm, wk),
                (wv_hbm, wv),
                (cot_hbm, ds_scr.at[:, 0:D]),
                (wo_hbm, wo),
                (wq_hbm, wq),
            )
        )
    ]
    for copy in loads:
        copy.start()
    barrier = pltpu.get_barrier_semaphore()
    peers = [sibling] + [f(n) for f in (y_peer, x_peer, z_peer) for n in (1, 2, 3)]
    for peer in peers:
        pl.semaphore_signal(barrier, inc=1, device_id=peer, device_id_type=MESH)

    def remote(src, dst, send, recv, peer):
        return pltpu.make_async_remote_copy(
            src_ref=src, dst_ref=dst, send_sem=send, recv_sem=recv, device_id=peer, device_id_type=MESH
        )

    def ds(start, size, step):
        return pl.ds(pl.multiple_of(start, step), size)

    def far_copy(p, n, src):
        return remote(far.at[src, p], far.at[src, p], far_s.at[n - 1, p], far_r.at[n - 1, p], y_peer(n))

    def df_copy(p, n):
        block = dfs.at[lax.rem(p, 2), lax.rem(y + n, 4)]
        return remote(block, dfr.at[p, n - 1], df_s.at[n - 1, p], df_r.at[n - 1, p], y_peer(n))

    def a_copy(p):
        block = part.at[lax.rem(p, 2), ds((1 - core) * HALF, HALF, HALF)]
        return remote(block, ar.at[p], a_s.at[p], a_r.at[p], sibling)

    def b_copy(p, n):
        block = bs.at[lax.rem(p, 2), ds(lax.rem(y + n, 4) * QUARTER, QUARTER, QUARTER)]
        return remote(block, br.at[p, n - 1], b_s.at[n - 1, p], b_r.at[n - 1, p], y_peer(n))

    def x_copy(p, n):
        block = cs.at[lax.rem(p, 2), ds(lax.rem(xi + n, 4) * PIECE, PIECE, PIECE)]
        return remote(block, xr.at[p, n - 1], x_s.at[n - 1, p], x_r.at[n - 1, p], x_peer(n))

    def z_copy(p, n, src):
        return remote(zr.at[p, src], zr.at[p, src], z_s.at[n - 1, p], z_r.at[n - 1, p], z_peer(n))

    def gx_copy(p, n, src):
        block = total.at[p, ds(core * HALF + y * QUARTER + src * PIECE, PIECE, PIECE)]
        return remote(fin.at[p], block, gx_s.at[n - 1, p], gx_r.at[n - 1, p], x_peer(n))

    def gl_copy(p):
        block = total.at[p, ds(core * HALF + y * QUARTER + xi * PIECE, PIECE, PIECE)]
        return pltpu.make_async_copy(fin.at[p], block, gl_s.at[p])

    def gy_copy(p, n, src):
        block = total.at[p, ds(core * HALF + src * QUARTER, QUARTER, QUARTER)]
        return remote(block, block, gy_s.at[n - 1, p], gy_r.at[n - 1, p], y_peer(n))

    def gc_copy(p, src):
        block = total.at[p, ds(src * HALF, HALF, HALF)]
        return remote(block, block, gc_s.at[p], gc_r.at[p], sibling)

    def back(index, n):
        return lax.rem(index + 4 - n, 4)

    pick = selection(False)
    left = lax.broadcasted_iota(jnp.int32, (128, 128), 1) < HEAD

    def spread(ref, j, value):
        for c in range(4):
            ref[c * FAR + j * 128 : c * FAR + j * 128 + 128, :] = value[c * 128 : c * 128 + 128]

    loads[0].wait()
    loads[1].wait()
    loads[2].wait()
    rows = []
    for j in range(2):
        block = nn(pick, e_scr[j * 512 : j * 512 + 512, 0:D]).astype(BF)
        rows.append(block)
        for n, (w, ref) in enumerate(((wk, k), (wv, v))):
            value = nn(block, w[...]).astype(BF)
            spread(ref, j, value)
            for t in range(PAIRS):
                c = 256 * (t % 2)
                at = slice(t * 128, t * 128 + 128)
                far[y, t, n, j * 128 : j * 128 + 128, :] = jnp.where(
                    left, value[c : c + 128, at], value[c + 128 : c + 256, at]
                )
    pl.semaphore_wait(barrier, len(peers))
    for p in range(PAIRS):
        for n in (1, 2, 3):
            far_copy(p, n, y).start()
    loads[3].wait()
    loads[4].wait()
    loads[5].wait()
    for j in range(2):
        spread(q, j, (nn(rows[j], wq[...]) * QUERY_SCALE).astype(BF))
        blockT = rows[j].T
        for c in range(4):
            xpT[:, c * FAR + j * 128 : c * FAR + j * 128 + 128] = blockT[:, c * 128 : c * 128 + 128]
        block = nn(pick, ds_scr[j * 512 : j * 512 + 512, 0:D]).astype(BF)
        spread(cp, j, block)
        spread(do, j, nt(block, wo[...]).astype(BF))

    zero, one = jnp.zeros((), BF), jnp.ones((), BF)

    def prepare(i):
        at = ds(i * 128, 128, 128)
        for n in (1, 2, 3):
            far_copy(i, n, back(y, n)).wait_recv()
        t_scr[2] = do[:, at].T
        t_scr[4] = q[:, at].T
        t_scr[5] = k[:, at].T
        t_scr[6] = v[:, at].T
        for s in range(4):
            t_scr[7, :, s * FAR : s * FAR + FAR] = far[s, i, 0].T
            t_scr[8, :, s * FAR : s * FAR + FAR] = far[s, i, 1].T

    def attend(i, a):
        slot = lax.rem(i, 2)
        lanes = ds(i * 128, 128, 128)
        lane = lax.broadcasted_iota(jnp.int32, (ROWS, 128), 1)
        row = lax.broadcasted_iota(jnp.int32, (ROWS, 128), 0)
        sub = lax.broadcasted_iota(jnp.int32, (128, ROWS), 0)
        near_bias = jnp.where(4 * (row & 255) + (row >> 8) + base < length, 0.0, NEGATIVE).astype(BF)
        rq = lax.broadcasted_iota(jnp.int32, (1, ROWS), 1)
        real = jnp.where(4 * (rq & 255) + (rq >> 8) + base < length, 1.0, 0.0)
        tail = jnp.where(lax.broadcasted_iota(jnp.int32, (16, ROWS), 0) == 0, 1.0, 0.0).astype(BF)
        o = HEAD * (1 - a)
        c = 2 * lax.rem(i, 2) + a
        mine = (lane < HEAD) if a == 0 else (lane >= HEAD)
        mine_t = (sub < HEAD) if a == 0 else (sub >= HEAD)
        sl = slice(HEAD * a, HEAD * a + HEAD)
        far_bias = jnp.where(4 * row + c < length, 0.0, NEGATIVE).astype(BF)
        ones2 = jnp.where((lane == o) | (lane == o + 1), one, zero)
        kf = far[:, i, 0].reshape(ROWS, 128)
        vf = far[:, i, 1].reshape(ROWS, 128)
        ka = jnp.where(mine, k[:, lanes], jnp.where(lane == o, near_bias, zero))
        kfa = jnp.where(mine, kf, jnp.where(lane == o, far_bias, zero))
        va = jnp.where(mine, v[:, lanes], ones2)
        vfa = jnp.where(mine, vf, ones2)
        t_scr[1] = jnp.where(mine_t, t_scr[4], jnp.where(sub == o, one, zero))
        t_scr[3, 0:1, :] = real.astype(BF)
        vta = jnp.concatenate([t_scr[6, sl, :], tail], axis=0)
        vfta = jnp.concatenate([t_scr[8, sl, :], tail], axis=0)
        kta, kfta = t_scr[5, sl, :], t_scr[7, sl, :]
        for b in range(4):
            at = ds(lax.rem(c + b, 4) * 256, 256, 256)
            qb = t_scr[1, :, at]
            s = nn(ka, qb)
            peak = jnp.max(s, axis=0, keepdims=True)
            if b == 0:
                sf = nn(kfa, qb)
                peak = jnp.maximum(peak, jnp.max(sf, axis=0, keepdims=True))
            e = jnp.exp2(s - peak).astype(BF)
            out = nn(vta, e)
            if b == 0:
                ef = jnp.exp2(sf - peak).astype(BF)
                out = out + nn(vfta, ef)
            weight = t_scr[3, 0:1, at].astype(F32) / out[HEAD : HEAD + 1]
            cx = (out[:HEAD] * weight).astype(BF)
            ctxT[i, sl, at] = cx
            dob = t_scr[2, sl, at].astype(F32)
            shift = -weight * jnp.sum(cx.astype(F32) * dob, axis=0, keepdims=True)
            high = shift.astype(BF)
            low = (shift - high.astype(F32)).astype(BF)
            dw = (dob * weight).astype(BF)
            sub2 = lax.broadcasted_iota(jnp.int32, (HEAD, 256), 0)
            extra = jnp.where(sub2 == 0, high, jnp.where(sub2 == 1, low, zero))
            dwa = jnp.concatenate([dw, extra] if a == 0 else [extra, dw], axis=0)
            dsc = e * nn(va, dwa).astype(BF)
            dq = nn(kta, dsc)
            if b == 0:
                dsf = ef * nn(vfa, dwa).astype(BF)
                dq = dq + nn(kfta, dsf)
                dfk = (nt(qb[sl], dsf) * LN2).astype(BF)
                dfv = nt(dw, ef).astype(BF)
                for j in range(4):
                    dfs[slot, j, 0, sl, :] = dfk[:, j * FAR : j * FAR + FAR]
                    dfs[slot, j, 1, sl, :] = dfv[:, j * FAR : j * FAR + FAR]
            dqT[i, sl, at] = (dq * 0.125).astype(BF)
            e_scr[:, at] = e
            ds_scr[:, at] = dsc
            t_scr[0, sl, at] = dw
        near[slot, 0, sl, :] = nt(t_scr[1, sl, :], ds_scr[...]) * LN2
        near[slot, 1, sl, :] = nt(t_scr[0, sl, :], e_scr[...])

    def send_far_grads(p):
        for n in (1, 2, 3):
            df_copy(p, n).start()

    def weigh(p):
        slot = lax.rem(p, 2)
        for n in (1, 2, 3):
            df_copy(p, n).wait()
        for a in range(2):
            sl = slice(HEAD * a, HEAD * a + HEAD)
            at = ds((2 * slot + a) * FAR, FAR, FAR)
            for n, dst in ((0, dkT), (1, dvT)):
                own = dfs[slot, y, n, sl, :].astype(F32)
                for m in range(3):
                    own = own + dfr[p, m, n, sl, :].astype(F32)
                dst[p, sl, :] = near[slot, n, sl, :].astype(BF)
                dst[p, sl, at] = (near[slot, n, sl, at] + own).astype(BF)
        for n, src in enumerate((dqT, dkT, dvT)):
            part[slot, n * D : n * D + D, :] = nt(xpT[...], src[p]).astype(BF)
        gout = nn(ctxT[p], cp[...]).astype(BF)
        for t in range(6):
            at = 3 * D + t * 128
            part[slot, at : at + 128, :] = gout[:, t * 128 : t * 128 + 128]
        a_copy(p).start()

    def sum_core(p):
        slot = lax.rem(p, 2)
        a_copy(p).wait()
        mine = part[slot, ds(core * HALF, HALF, HALF), :]
        bs[slot] = (mine.astype(F32) + ar[p].astype(F32)).astype(BF)
        for n in (1, 2, 3):
            b_copy(p, n).start()

    def sum_y(p):
        slot = lax.rem(p, 2)
        for n in (1, 2, 3):
            b_copy(p, n).wait()
        acc = bs[slot, ds(y * QUARTER, QUARTER, QUARTER), :].astype(F32)
        for n in range(3):
            acc = acc + br[p, n].astype(F32)
        cs[slot] = acc.astype(BF)
        for n in (1, 2, 3):
            x_copy(p, n).start()

    def sum_x(p):
        slot = lax.rem(p, 2)
        for n in (1, 2, 3):
            x_copy(p, n).wait()
        acc = cs[slot, ds(xi * PIECE, PIECE, PIECE), :].astype(F32)
        for n in range(3):
            acc = acc + xr[p, n].astype(F32)
        zr[p, zi] = acc.astype(BF)
        for n in (1, 2, 3):
            z_copy(p, n, zi).start()

    def sum_z(p):
        for n in (1, 2, 3):
            z_copy(p, n, zi).wait_send()
            z_copy(p, n, back(zi, n)).wait_recv()
        acc = zr[p, 0].astype(F32)
        for n in (1, 2, 3):
            acc = acc + zr[p, n].astype(F32)
        fin[p] = acc.astype(BF)
        gl_copy(p).start()
        for n in (1, 2, 3):
            gx_copy(p, n, xi).start()

    def gather_y(p):
        gl_copy(p).wait()
        for n in (1, 2, 3):
            gx_copy(p, n, xi).wait_send()
            gx_copy(p, n, back(xi, n)).wait_recv()
        for n in (1, 2, 3):
            gy_copy(p, n, y).start()

    def gather_core(p):
        for n in (1, 2, 3):
            gy_copy(p, n, y).wait_send()
            gy_copy(p, n, back(y, n)).wait_recv()
        gc_copy(p, core).start()

    def end(p):
        gc_copy(p, core).wait_send()
        gc_copy(p, 1 - core).wait_recv()

    first = ((weigh, 1), (sum_y, 2), (sum_z, 3), (gather_core, 4))
    second = ((sum_core, 1), (sum_x, 2), (gather_y, 3), (end, 4))

    def step(i, carry):
        prepare(i)
        attend(i, 0)
        for run, lag in first:
            pl.when(i >= lag)(lambda run=run, lag=lag: run(i - lag))
        attend(i, 1)
        send_far_grads(i)
        for run, lag in second:
            pl.when(i >= lag)(lambda run=run, lag=lag: run(i - lag))
        return carry

    lax.fori_loop(0, PAIRS, step, 0)

    place = selection(True)

    def cols(ref, j):
        return jnp.concatenate(
            [ref[:, :, c * FAR + j * 128 : c * FAR + j * 128 + 128].reshape(D, 128) for c in range(4)], axis=1
        )

    def attended(j):
        outT = nn(wo[...].T, cols(ctxT, j)).astype(BF)
        q[j * 512 : j * 512 + 512, :] = nt(place, outT).astype(BF)

    def patch_grads(j):
        gT = nn(wq[...], cols(dqT, j)) + nn(wk[...], cols(dkT, j)) + nn(wv[...], cols(dvT, j))
        k[j * 512 : j * 512 + 512, :] = nt(place, gT.astype(BF)).astype(BF)

    att_copy = pltpu.make_async_copy(q, att_hbm, out_sem.at[0])
    grad_copy = pltpu.make_async_copy(k, gx_hbm, out_sem.at[1])

    sum_y(4)
    sum_z(3)
    gather_core(2)
    attended(0)
    weigh(5)
    sum_x(4)
    gather_y(3)
    end(2)
    attended(1)
    att_copy.start()
    sum_core(5)
    sum_z(4)
    gather_core(3)
    patch_grads(0)
    sum_y(5)
    gather_y(4)
    end(3)
    patch_grads(1)
    grad_copy.start()
    sum_x(5)
    gather_core(4)
    sum_z(5)
    end(4)
    gather_y(5)
    gather_core(5)
    end(5)
    att_copy.wait()
    grad_copy.wait()
    for p in range(PAIRS):
        for n in (1, 2, 3):
            far_copy(p, n, y).wait_send()


def sublayer(info, x, cot, wq, wk, wv, wo):
    anywhere = pl.BlockSpec(memory_space=pl.ANY)
    dma = pltpu.SemaphoreType.DMA
    three, each = dma((3, PAIRS)), dma((PAIRS,))
    scratch = [
        *[pltpu.VMEM((D, D), BF)] * 4,
        pltpu.VMEM((D, ROWS), BF),
        pltpu.VMEM((ROWS, D), BF),
        *[pltpu.VMEM((ROWS, D), BF)] * 4,
        pltpu.VMEM((4, PAIRS, 2, FAR, 128), BF),
        *[pltpu.VMEM((PAIRS, 128, ROWS), BF)] * 4,
        pltpu.VMEM((ROWS, ROWS), BF),
        pltpu.VMEM((ROWS, ROWS), BF),
        pltpu.VMEM((9, 128, ROWS), BF),
        pltpu.VMEM((2, 2, 128, ROWS), F32),
        pltpu.VMEM((2, 4, 2, 128, FAR), BF),
        pltpu.VMEM((PAIRS, 3, 2, 128, FAR), BF),
        pltpu.VMEM((2, PART, 128), BF),
        pltpu.VMEM((PAIRS, HALF, 128), BF),
        pltpu.VMEM((2, HALF, 128), BF),
        pltpu.VMEM((PAIRS, 3, QUARTER, 128), BF),
        pltpu.VMEM((2, QUARTER, 128), BF),
        pltpu.VMEM((PAIRS, 3, PIECE, 128), BF),
        pltpu.VMEM((PAIRS, 4, PIECE, 128), BF),
        pltpu.VMEM((PAIRS, PIECE, 128), BF),
        dma((6,)),
        three, three, three, three, each, each, three, three, three, three, three, three,
        three, three, each, three, three, each, each, dma((2,)),
    ]
    return pl.pallas_call(
        kernel,
        in_specs=[pl.BlockSpec(memory_space=pltpu.SMEM)] + [anywhere] * 6,
        out_specs=[anywhere] * 3,
        out_shape=[
            jax.ShapeDtypeStruct((ROWS, D), BF),
            jax.ShapeDtypeStruct((ROWS, D), BF),
            jax.ShapeDtypeStruct((PAIRS, PART, 128), BF),
        ],
        scratch_shapes=scratch,
        compiler_params=pltpu.CompilerParams(
            vmem_limit_bytes=VMEM_LIMIT, collective_id=0, has_side_effects=True
        ),
    )(info, x, cot, wq, wk, wv, wo)


def local(patches, wq, wk, wv, wo, lengths, cotangent):
    att, gx, total = sublayer(lengths, patches[0], cotangent[0], wq, wk, wv, wo)
    columns = [
        total[:, n * D : n * D + D].transpose(1, 0, 2).reshape(D, D) for n in range(3)
    ]
    rows = total[:, 3 * D :].reshape(PAIRS, PAIRS, 128, 128).transpose(0, 2, 1, 3).reshape(D, D)
    return (att[None], gx[None], *columns, rows)


def solution(mesh):
    split = P("slide", "seq", None)
    return jax.shard_map(
        local,
        mesh=mesh,
        in_specs=(split, P(), P(), P(), P(), P("slide"), split),
        out_specs=(split, split, P(), P(), P(), P()),
        check_vma=False,
    )
```

time: 340 us -> 211 us (0.62)
  blocking collectives: 113 us -> 0 us
  waiting for transfers between devices: 80.1 us -> 0 us
  Pallas kernels: 122 us -> 193 us
  between operations: 14.7 us -> 1.32 us
  local copies, waits for them, and re-layouts: 7.98 us -> 16.6 us
    psum x1 -> x0, blocking collectives: 113 us -> none  [local(): totals = lax.psum(grads, ('seq', 'slide')).astype(BF)]
    pallas_call x3 -> x1, Pallas kernels: 122 us -> 193 us  [sublayer(): pl.pallas_call(kernel, in_specs=[pl.BlockSpec(memory_space=pltpu.SMEM)] +...]
    all_gather x1 -> x0, waiting for transfers between devices: 41.5 us -> none  [local(): far_all = lax.all_gather(far, 'seq', axis=0)]
    reduce_scatter x1 -> x0, waiting for transfers between devices: 38.6 us -> none  [local(): own = lax.psum_scatter(dfar, 'seq', scatter_dimension=0, tiled=False)]
    unnamed x3 -> x8, local copies, waits for them, and re-layouts: 4.32 us -> 10.4 us
    squeeze x1 -> x0, local copies, waits for them, and re-layouts: 3.65 us -> none  [local(): totals[3]]
  transfers between devices with their start and end apart: 2 -> 0, of which waited for: 2 -> 0; matrix products, arithmetic and copies ran while one was open for 0% -> 0% of each run, Pallas kernels for 0% -> 0%
where the time goes in v2:
time: 211 us
  Pallas kernels  193 us (91%)
  local copies, waits for them, and re-layouts  16.6 us (8%)
    pallas_call x1, Pallas kernels, sublayer(): pl.pallas_call(kernel, in_specs=[pl.BlockSpec(memory_space=pltpu.SMEM)] +...  193 us
    unnamed x8, local copies, waits for them, and re-layouts  10.4 us

profile of v2, /device:TPU:1, one launch (start us, length us, event | category | flops | bytes accessed | tf_op | source)
XLA Modules:
  0.0 211.2 jit_solution(3613210496476858497)
XLA Ops:
  1.3 193.3 %shard_map.118 = (bf16[1024,768]{1,0:T(8,128)(2,1)}, bf16[1024,768]{1,0:T(8,128)(2,1)}, bf16[6,3072,128]{2,1,0:T(8,128)(2,1)}) custom-call(s32[1]{0:T(128)S(6)} %copy.26.info, bf16[1024,768]{1,0:T(8,128)(2,1)} %bitcast.27, bf16[1024,768]{1,0:T(8,128)(2,1)} %bitcast.28, bf16[768,768]{1,0:T(8,128)(2,1)} %wq_hbm.1, bf16[768,768]{1,0:T(8,128)(2,1)} %wk_hbm.1, ...), custom_call_target="tpu_custom_call" | custom-call | tf_op jit(solution)/shard_map/pallas_call | solution.py:435
  194.6 2.8 %fusion = (bf16[6,768,128]{2,1,0:T(8,128)(2,1)S(1)}, bf16[768,6,128]{2,0,1:T(8,128)(2,1)S(1)}, bf16[768,6,128]{2,0,1:T(8,128)(2,1)S(1)}, bf16[768,6,128]{2,0,1:T(8,128)(2,1)S(1)}) fusion(bf16[6,3072,128]{2,1,0:T(8,128)(2,1)} %get-tuple-element.11), kind=kLoop, calls=%fused_computation.4 | loop fusion | bytes 9437184 | tf_op jit(solution)/shard_map/slice | solution.py:456
  197.4 0.8 copy.17
  198.2 1.2 copy.23
  199.4 1.4 copy.16
  200.8 2.4 %copy.20 = bf16[768,768]{1,0:T(8,128)(2,1)} copy(bf16[768,768]{0,1:T(8,128)(2,1)} %bitcast.22) | data formatting | bytes 2359296
  203.2 0.6 copy.15
  203.8 1.5 copy.19
  205.3 0.6 copy.14
  205.9 1.5 copy.18
  207.3 0.0 copy-start
  207.3 2.8 %copy.27 = bf16[1,1024,768]{2,1,0:T(8,128)(2,1)} copy(bf16[1,1024,768]{2,1,0:T(8,128)(2,1)} %bitcast.26) | data formatting | bytes 3145728
  210.1 0.0 copy-done
  210.1 1.1 copy.28
Async XLA Ops:
  207.3 2.8 %copy-start = (bf16[1024,768]{1,0:T(8,128)(2,1)S(1)}, bf16[1024,768]{1,0:T(8,128)(2,1)}, u32[]{:S(2)}) copy-start(bf16[1024,768]{1,0:T(8,128)(2,1)} %get-tuple-element.10) | copy-start | bytes 4718596

commit v3 on v2

v3 whole, which is shorter than its diff:
```python
import math

import jax
import jax.numpy as jnp
from jax import lax
from jax.experimental import pallas as pl
from jax.experimental.pallas import tpu as pltpu
from jax.sharding import PartitionSpec as P

BF, F32 = jnp.bfloat16, jnp.float32
MESH = pl.DeviceIdType.MESH
NEGATIVE = -1e30
ROWS, D, HEAD, PAIRS = 1024, 768, 64, 6
FAR = 256
LN2 = math.log(2.0)
QUERY_SCALE = 1.0 / (math.sqrt(HEAD) * LN2)
VMEM_LIMIT = 60 << 20
PART, HALF, PIECE = 3072, 1536, 96
PLANE = 16


def nn(a, b):
    return lax.dot_general(a, b, (((1,), (0,)), ((), ())), preferred_element_type=F32)


def nt(a, b):
    return lax.dot_general(a, b, (((1,), (1,)), ((), ())), preferred_element_type=F32)


def selection(transposed):
    a = lax.broadcasted_iota(jnp.int32, (512, 512), 1 if transposed else 0)
    b = lax.broadcasted_iota(jnp.int32, (512, 512), 0 if transposed else 1)
    return jnp.where(4 * (a & 127) + (a >> 7) == b, 1.0, 0.0).astype(BF)


def kernel(
    info, x_hbm, cot_hbm, wq_hbm, wk_hbm, wv_hbm, wo_hbm,
    att_hbm, gx_hbm, total,
    wq, wk, wv, wo, xpT, cp, q, k, v, do, far,
    ctxT, dqT, dkT, dvT, e_scr, ds_scr, t_scr, o_scr, near,
    dfs, dfr, part, ar, bs, br, yr, fin,
    load_sem, far_s, far_r, df_s, df_r, a_s, a_r, b_s, b_r, y_s, y_r,
    g_s, g_r, gl_s, gc_s, gc_r, out_sem,
):
    y = lax.axis_index("seq").astype(jnp.int32)
    slide = lax.axis_index("slide").astype(jnp.int32)
    spot = lax.div(slide, 2)
    core = lax.rem(slide, 2)
    length = info[0]
    base = y * ROWS

    def y_peer(n):
        return (lax.rem(y + n, 4), slide)

    def plane_peer(n):
        return (y, 2 * lax.rem(spot + n, PLANE) + core)

    sibling = (y, slide + 1 - 2 * core)

    loads = [
        pltpu.make_async_copy(src, dst, load_sem.at[n])
        for n, (src, dst) in enumerate(
            (
                (x_hbm, e_scr.at[:, 0:D]),
                (wk_hbm, wk),
                (wv_hbm, wv),
                (cot_hbm, ds_scr.at[:, 0:D]),
                (wo_hbm, wo),
                (wq_hbm, wq),
            )
        )
    ]
    for copy in loads:
        copy.start()
    barrier = pltpu.get_barrier_semaphore()
    peers = [sibling] + [y_peer(n) for n in (1, 2, 3)] + [plane_peer(n) for n in range(1, PLANE)]
    for peer in peers:
        pl.semaphore_signal(barrier, inc=1, device_id=peer, device_id_type=MESH)

    def remote(src, dst, send, recv, peer):
        return pltpu.make_async_remote_copy(
            src_ref=src, dst_ref=dst, send_sem=send, recv_sem=recv, device_id=peer, device_id_type=MESH
        )

    def ds(start, size, step):
        return pl.ds(pl.multiple_of(start, step), size)

    def far_copy(p, n, src):
        return remote(far.at[src, p], far.at[src, p], far_s.at[n - 1, p], far_r.at[n - 1, p], y_peer(n))

    def df_copy(p, a, n):
        block = dfs.at[lax.rem(p, 2), a, lax.rem(y + n, 4)]
        return remote(block, dfr.at[p, a, n - 1], df_s.at[a, n - 1, p], df_r.at[a, n - 1, p], y_peer(n))

    def a_copy(p):
        block = part.at[lax.rem(p, 2), ds((1 - core) * HALF, HALF, HALF)]
        return remote(block, ar.at[p], a_s.at[p], a_r.at[p], sibling)

    def b_copy(p, n):
        block = bs.at[lax.rem(p, 2), ds(lax.rem(spot + n, PLANE) * PIECE, PIECE, PIECE)]
        return remote(block, br.at[p, n - 1], b_s.at[p], b_r.at[p], plane_peer(n))

    def b_all(p):
        block = br.at[p]
        return remote(block, block, b_s.at[p], b_r.at[p], sibling)

    def y_copy(p, n, src):
        return remote(yr.at[p, src], yr.at[p, src], y_s.at[n - 1, p], y_r.at[n - 1, p], y_peer(n))

    def g_copy(p, n):
        block = total.at[p, ds(core * HALF + spot * PIECE, PIECE, PIECE)]
        return remote(fin.at[p], block, g_s.at[p], g_r.at[p], plane_peer(n))

    def g_all(p):
        block = total.at[p, 0 : HALF - PIECE]
        return remote(block, block, g_s.at[p], g_r.at[p], sibling)

    def gl_copy(p):
        block = total.at[p, ds(core * HALF + spot * PIECE, PIECE, PIECE)]
        return pltpu.make_async_copy(fin.at[p], block, gl_s.at[p])

    def gc_copy(p, src):
        block = total.at[p, ds(src * HALF, HALF, HALF)]
        return remote(block, block, gc_s.at[p], gc_r.at[p], sibling)

    def to_plane(copy, p):
        def one(n, carry):
            copy(p, n).start()
            return carry

        lax.fori_loop(1, PLANE, one, 0)

    def back(index, n):
        return lax.rem(index + 4 - n, 4)

    def send_far(p):
        for n in (1, 2, 3):
            far_copy(p, n, y).start()

    pick = selection(False)
    left = lax.broadcasted_iota(jnp.int32, (128, 128), 1) < HEAD

    def spread(ref, j, value):
        for c in range(4):
            ref[c * FAR + j * 128 : c * FAR + j * 128 + 128, :] = value[c * 128 : c * 128 + 128]

    loads[0].wait()
    loads[1].wait()
    loads[2].wait()
    rows = []
    for j in range(2):
        block = nn(pick, e_scr[j * 512 : j * 512 + 512, 0:D]).astype(BF)
        rows.append(block)
        for n, (w, ref) in enumerate(((wk, k), (wv, v))):
            value = nn(block, w[...]).astype(BF)
            spread(ref, j, value)
            for t in range(PAIRS):
                c = 256 * (t % 2)
                at = slice(t * 128, t * 128 + 128)
                far[y, t, n, j * 128 : j * 128 + 128, :] = jnp.where(
                    left, value[c : c + 128, at], value[c + 128 : c + 256, at]
                )
    pl.semaphore_wait(barrier, len(peers))
    send_far(0)
    loads[3].wait()
    loads[4].wait()
    loads[5].wait()
    for j in range(2):
        spread(q, j, (nn(rows[j], wq[...]) * QUERY_SCALE).astype(BF))
        blockT = rows[j].T
        for c in range(4):
            xpT[:, c * FAR + j * 128 : c * FAR + j * 128 + 128] = blockT[:, c * 128 : c * 128 + 128]
        block = nn(pick, ds_scr[j * 512 : j * 512 + 512, 0:D]).astype(BF)
        spread(cp, j, block)
        spread(do, j, nt(block, wo[...]).astype(BF))

    send_far(1)
    zero, one = jnp.zeros((), BF), jnp.ones((), BF)

    def prepare(i):
        at = ds(i * 128, 128, 128)
        t_scr[2] = do[:, at].T
        t_scr[4] = q[:, at].T
        t_scr[5] = k[:, at].T
        t_scr[6] = v[:, at].T

    def receive(i):
        for n in (1, 2, 3):
            far_copy(i, n, back(y, n)).wait_recv()
        for s in range(4):
            t_scr[7, :, s * FAR : s * FAR + FAR] = far[s, i, 0].T
            t_scr[8, :, s * FAR : s * FAR + FAR] = far[s, i, 1].T

    def attend(i, a):
        slot = lax.rem(i, 2)
        lanes = ds(i * 128, 128, 128)
        lane = lax.broadcasted_iota(jnp.int32, (ROWS, 128), 1)
        row = lax.broadcasted_iota(jnp.int32, (ROWS, 128), 0)
        sub = lax.broadcasted_iota(jnp.int32, (128, ROWS), 0)
        near_bias = jnp.where(4 * (row & 255) + (row >> 8) + base < length, 0.0, NEGATIVE).astype(BF)
        rq = lax.broadcasted_iota(jnp.int32, (1, ROWS), 1)
        real = jnp.where(4 * (rq & 255) + (rq >> 8) + base < length, 1.0, 0.0)
        tail = jnp.where(lax.broadcasted_iota(jnp.int32, (16, ROWS), 0) == 0, 1.0, 0.0).astype(BF)
        o = HEAD * (1 - a)
        c = 2 * lax.rem(i, 2) + a
        mine = (lane < HEAD) if a == 0 else (lane >= HEAD)
        mine_t = (sub < HEAD) if a == 0 else (sub >= HEAD)
        sl = slice(HEAD * a, HEAD * a + HEAD)
        far_bias = jnp.where(4 * row + c < length, 0.0, NEGATIVE).astype(BF)
        ones2 = jnp.where((lane == o) | (lane == o + 1), one, zero)
        ka = jnp.where(mine, k[:, lanes], jnp.where(lane == o, near_bias, zero))
        va = jnp.where(mine, v[:, lanes], ones2)
        t_scr[1] = jnp.where(mine_t, t_scr[4], jnp.where(sub == o, one, zero))
        vta = jnp.concatenate([t_scr[6, sl, :], tail], axis=0)
        own = ds(c * FAR, FAR, FAR)
        for b in (1, 2, 3):
            at = ds(lax.rem(c + b, 4) * FAR, FAR, FAR)
            s = nn(ka, t_scr[1, :, at])
            e_scr[:, at] = jnp.exp2(s - jnp.max(s, axis=0, keepdims=True)).astype(BF)
        if a == 0:
            receive(i)
        kfa = jnp.where(mine, far[:, i, 0].reshape(ROWS, 128), jnp.where(lane == o, far_bias, zero))
        vfa = jnp.where(mine, far[:, i, 1].reshape(ROWS, 128), ones2)
        qc = t_scr[1, :, own]
        sf = nn(kfa, qc)
        s = nn(ka, qc)
        peak = jnp.maximum(jnp.max(s, axis=0, keepdims=True), jnp.max(sf, axis=0, keepdims=True))
        e_scr[:, own] = jnp.exp2(s - peak).astype(BF)
        ef = jnp.exp2(sf - peak).astype(BF)
        o_scr[...] = nn(vta, e_scr[...])
        o_scr[:, own] = o_scr[:, own] + nn(jnp.concatenate([t_scr[8, sl, :], tail], axis=0), ef)
        weight = real / o_scr[HEAD : HEAD + 1]
        cx = (o_scr[:HEAD] * weight).astype(BF)
        ctxT[i, sl, :] = cx
        dob = t_scr[2, sl, :].astype(F32)
        shift = -weight * jnp.sum(cx.astype(F32) * dob, axis=0, keepdims=True)
        high = shift.astype(BF)
        low = (shift - high.astype(F32)).astype(BF)
        sub2 = lax.broadcasted_iota(jnp.int32, (HEAD, ROWS), 0)
        t_scr[0, sl, :] = (dob * weight).astype(BF)
        t_scr[0, o : o + HEAD, :] = jnp.where(sub2 == 0, high, jnp.where(sub2 == 1, low, zero))
        dwc = t_scr[0, :, own]
        dsf = ef * nn(vfa, dwc).astype(BF)
        dfk = (nt(qc[sl], dsf) * LN2).astype(BF)
        dfv = nt(dwc[sl], ef).astype(BF)
        for j in range(4):
            dfs[slot, a, j, 0] = dfk[:, j * FAR : j * FAR + FAR]
            dfs[slot, a, j, 1] = dfv[:, j * FAR : j * FAR + FAR]
        for n in (1, 2, 3):
            df_copy(i, a, n).start()
        for b in range(4):
            at = slice(b * FAR, b * FAR + FAR)
            ds_scr[:, at] = e_scr[:, at] * nn(va, t_scr[0, :, at]).astype(BF)
        o_scr[:HEAD] = nn(t_scr[5, sl, :], ds_scr[...])
        o_scr[:HEAD, own] = o_scr[:HEAD, own] + nn(t_scr[7, sl, :], dsf)
        dqT[i, sl, :] = (o_scr[:HEAD] * 0.125).astype(BF)
        near[slot, 0, sl, :] = nt(t_scr[1, sl, :], ds_scr[...]) * LN2
        near[slot, 1, sl, :] = nt(t_scr[0, sl, :], e_scr[...])

    def weigh(p):
        slot = lax.rem(p, 2)
        for a in range(2):
            for n in (1, 2, 3):
                df_copy(p, a, n).wait()
            sl = slice(HEAD * a, HEAD * a + HEAD)
            at = ds((2 * slot + a) * FAR, FAR, FAR)
            for n, dst in ((0, dkT), (1, dvT)):
                own = dfs[slot, a, y, n].astype(F32)
                for m in range(3):
                    own = own + dfr[p, a, m, n].astype(F32)
                dst[p, sl, :] = near[slot, n, sl, :].astype(BF)
                dst[p, sl, at] = (near[slot, n, sl, at] + own).astype(BF)
        for n, src in enumerate((dqT, dkT, dvT)):
            part[slot, n * D : n * D + D, :] = nt(xpT[...], src[p]).astype(BF)
        gout = nn(ctxT[p], cp[...]).astype(BF)
        for t in range(6):
            at = 3 * D + t * 128
            part[slot, at : at + 128, :] = gout[:, t * 128 : t * 128 + 128]
        a_copy(p).start()

    def sum_core(p):
        slot = lax.rem(p, 2)
        a_copy(p).wait()
        mine = part[slot, ds(core * HALF, HALF, HALF), :]
        bs[slot] = (mine.astype(F32) + ar[p].astype(F32)).astype(BF)
        to_plane(b_copy, p)

    def sum_plane(p):
        b_all(p).wait()
        acc = bs[lax.rem(p, 2), ds(spot * PIECE, PIECE, PIECE), :].astype(F32)
        for n in range(PLANE - 1):
            acc = acc + br[p, n].astype(F32)
        yr[p, y] = acc.astype(BF)
        for n in (1, 2, 3):
            y_copy(p, n, y).start()

    def sum_y(p):
        for n in (1, 2, 3):
            y_copy(p, n, y).wait_send()
            y_copy(p, n, back(y, n)).wait_recv()
        acc = yr[p, 0].astype(F32)
        for n in (1, 2, 3):
            acc = acc + yr[p, n].astype(F32)
        fin[p] = acc.astype(BF)
        gl_copy(p).start()
        to_plane(g_copy, p)

    def gather(p):
        gl_copy(p).wait()
        g_all(p).wait()
        gc_copy(p, core).start()

    def end(p):
        gc_copy(p, core).wait_send()
        gc_copy(p, 1 - core).wait_recv()

    first = ((weigh, 1), (sum_plane, 2), (gather, 3))
    second = ((sum_core, 1), (sum_y, 2), (end, 3))

    def step(i, carry):
        prepare(i)
        attend(i, 0)
        pl.when(i < PAIRS - 2)(lambda: send_far(i + 2))
        for run, lag in first:
            pl.when(i >= lag)(lambda run=run, lag=lag: run(i - lag))
        attend(i, 1)
        for run, lag in second:
            pl.when(i >= lag)(lambda run=run, lag=lag: run(i - lag))
        return carry

    lax.fori_loop(0, PAIRS, step, 0)

    place = selection(True)

    def cols(ref, j):
        return jnp.concatenate(
            [ref[:, :, c * FAR + j * 128 : c * FAR + j * 128 + 128].reshape(D, 128) for c in range(4)], axis=1
        )

    def attended(j):
        outT = nn(wo[...].T, cols(ctxT, j)).astype(BF)
        q[j * 512 : j * 512 + 512, :] = nt(place, outT).astype(BF)

    def patch_grads(j):
        gT = nn(wq[...], cols(dqT, j)) + nn(wk[...], cols(dkT, j)) + nn(wv[...], cols(dvT, j))
        k[j * 512 : j * 512 + 512, :] = nt(place, gT.astype(BF)).astype(BF)

    att_copy = pltpu.make_async_copy(q, att_hbm, out_sem.at[0])
    grad_copy = pltpu.make_async_copy(k, gx_hbm, out_sem.at[1])

    sum_plane(4)
    gather(3)
    attended(0)
    weigh(5)
    sum_y(4)
    end(3)
    attended(1)
    att_copy.start()
    sum_core(5)
    gather(4)
    patch_grads(0)
    sum_plane(5)
    end(4)
    patch_grads(1)
    grad_copy.start()
    sum_y(5)
    gather(5)
    end(5)
    att_copy.wait()
    grad_copy.wait()
    for p in range(PAIRS):
        for n in (1, 2, 3):
            far_copy(p, n, y).wait_send()


def sublayer(info, x, cot, wq, wk, wv, wo):
    anywhere = pl.BlockSpec(memory_space=pl.ANY)
    dma = pltpu.SemaphoreType.DMA
    three, each = dma((3, PAIRS)), dma((PAIRS,))
    scratch = [
        *[pltpu.VMEM((D, D), BF)] * 4,
        pltpu.VMEM((D, ROWS), BF),
        pltpu.VMEM((ROWS, D), BF),
        *[pltpu.VMEM((ROWS, D), BF)] * 4,
        pltpu.VMEM((4, PAIRS, 2, FAR, 128), BF),
        *[pltpu.VMEM((PAIRS, 128, ROWS), BF)] * 4,
        pltpu.VMEM((ROWS, ROWS), BF),
        pltpu.VMEM((ROWS, ROWS), BF),
        pltpu.VMEM((9, 128, ROWS), BF),
        pltpu.VMEM((HEAD + 16, ROWS), F32),
        pltpu.VMEM((2, 2, 128, ROWS), F32),
        pltpu.VMEM((2, 2, 4, 2, HEAD, FAR), BF),
        pltpu.VMEM((PAIRS, 2, 3, 2, HEAD, FAR), BF),
        pltpu.VMEM((2, PART, 128), BF),
        pltpu.VMEM((PAIRS, HALF, 128), BF),
        pltpu.VMEM((2, HALF, 128), BF),
        pltpu.VMEM((PAIRS, PLANE - 1, PIECE, 128), BF),
        pltpu.VMEM((PAIRS, 4, PIECE, 128), BF),
        pltpu.VMEM((PAIRS, PIECE, 128), BF),
        dma((6,)),
        three, three, dma((2, 3, PAIRS)), dma((2, 3, PAIRS)), each, each, each, each, three, three,
        each, each, each, each, each, dma((2,)),
    ]
    return pl.pallas_call(
        kernel,
        in_specs=[pl.BlockSpec(memory_space=pltpu.SMEM)] + [anywhere] * 6,
        out_specs=[anywhere] * 3,
        out_shape=[
            jax.ShapeDtypeStruct((ROWS, D), BF),
            jax.ShapeDtypeStruct((ROWS, D), BF),
            jax.ShapeDtypeStruct((PAIRS, PART, 128), BF),
        ],
        scratch_shapes=scratch,
        compiler_params=pltpu.CompilerParams(
            vmem_limit_bytes=VMEM_LIMIT, collective_id=0, has_side_effects=True
        ),
    )(info, x, cot, wq, wk, wv, wo)


def assemble_kernel(att, gx, total, att_out, gx_out, gq, gk, gv, go):
    att_out[...] = att[...]
    gx_out[...] = gx[...]
    for n, ref in enumerate((gq, gk, gv)):
        ref[...] = total[0, n * D : n * D + D, :]
    for t in range(PAIRS):
        go[:, t * 128 : t * 128 + 128] = total[0, 3 * D + t * 128 : 3 * D + t * 128 + 128, :]


def assemble(att, gx, total):
    rows, square = jax.ShapeDtypeStruct((ROWS, D), BF), jax.ShapeDtypeStruct((D, D), BF)
    wide = pl.BlockSpec((ROWS, 128), lambda p: (0, p))
    column = pl.BlockSpec((D, 128), lambda p: (0, p))
    return pl.pallas_call(
        assemble_kernel,
        grid=(PAIRS,),
        in_specs=[wide, wide, pl.BlockSpec((1, PART, 128), lambda p: (p, 0, 0))],
        out_specs=[wide, wide, column, column, column, pl.BlockSpec((128, D), lambda p: (p, 0))],
        out_shape=[rows, rows, square, square, square, square],
        compiler_params=pltpu.CompilerParams(vmem_limit_bytes=VMEM_LIMIT),
    )(att, gx, total)


def local(patches, wq, wk, wv, wo, lengths, cotangent):
    att, gx, total = sublayer(lengths, patches[0], cotangent[0], wq, wk, wv, wo)
    att, gx, *grads = assemble(att, gx, total)
    return (att[None], gx[None], *grads)


def solution(mesh):
    split = P("slide", "seq", None)
    return jax.shard_map(
        local,
        mesh=mesh,
        in_specs=(split, P(), P(), P(), P(), P("slide"), split),
        out_specs=(split, split, P(), P(), P(), P()),
        check_vma=False,
    )
```

time: 211 us -> 154 us (0.73)
  Pallas kernels: 193 us -> 153 us
  local copies, waits for them, and re-layouts: 16.6 us -> 0 us
    pallas_call x1, Pallas kernels: 193 us -> 145 us  [sublayer(): pl.pallas_call(kernel, in_specs=[pl.BlockSpec(memory_space=pltpu.SMEM)] +...]
    unnamed x8 -> x0, local copies, waits for them, and re-layouts: 10.4 us -> none
    pallas_call x0 -> x1, Pallas kernels: none -> 7.78 us  [assemble(): pl.pallas_call(assemble_kernel, grid=(PAIRS,), in_specs=[wide, wide, pl.B...]
    slice x1 -> x0, local copies, waits for them, and re-layouts: 2.79 us -> none  [local(): total[:, 3 * D:].reshape(PAIRS, PAIRS, 128, 128).transpose(0, 2, 1, 3)]
    transpose x3 -> x0, local copies, waits for them, and re-layouts: 2.59 us -> none  [local(): total[:, n * D:n * D + D].transpose(1, 0, 2).reshape(D, D)]
where the time goes in v3:
time: 154 us
  Pallas kernels  153 us (99%)
    pallas_call x1, Pallas kernels, sublayer(): pl.pallas_call(kernel, in_specs=[pl.BlockSpec(memory_space=pltpu.SMEM)] +...  145 us
    pallas_call x1, Pallas kernels, assemble(): pl.pallas_call(assemble_kernel, grid=(PAIRS,), in_specs=[wide, wide, pl.B...  7.78 us

profile of v3, /device:TPU:1, one launch (start us, length us, event | category | flops | bytes accessed | tf_op | source)
XLA Modules:
  0.0 154.1 jit_solution(9848434372842009499)
XLA Ops:
  1.3 145.0 %shard_map.118 = (bf16[1024,768]{1,0:T(8,128)(2,1)}, bf16[1024,768]{1,0:T(8,128)(2,1)}, bf16[6,3072,128]{2,1,0:T(8,128)(2,1)}) custom-call(s32[1]{0:T(128)S(6)} %copy.13.info, bf16[1024,768]{1,0:T(8,128)(2,1)} %bitcast.4, bf16[1024,768]{1,0:T(8,128)(2,1)} %bitcast.5, bf16[768,768]{1,0:T(8,128)(2,1)} %wq_hbm.1, bf16[768,768]{1,0:T(8,128)(2,1)} %wk_hbm.1, ...), custom_call_target="tpu_custom_call" | custom-call | tf_op jit(solution)/shard_map/pallas_call | solution.py:404
  146.3 7.8 %shard_map.119 = (bf16[1024,768]{1,0:T(8,128)(2,1)}, bf16[1024,768]{1,0:T(8,128)(2,1)}, bf16[768,768]{1,0:T(8,128)(2,1)}, bf16[768,768]{1,0:T(8,128)(2,1)}, bf16...) custom-call(bf16[1024,768]{1,0:T(8,128)(2,1)} %get-tuple-element.15.att, bf16[1024,768]{1,0:T(8,128)(2,1)} %get-tuple-element.16.gx, ...), custom_call_target="tpu_custom_call" | custom-call | tf_op jit(solution)/shard_map/pallas_call | solution.py:433

commit v4 on v3

--- a/solution.py
+++ b/solution.py
@@ -14,9 +14,10 @@
 FAR = 256
 LN2 = math.log(2.0)
 QUERY_SCALE = 1.0 / (math.sqrt(HEAD) * LN2)
-VMEM_LIMIT = 60 << 20
+VMEM_LIMIT = 62 << 20
 PART, HALF, PIECE = 3072, 1536, 96
 PLANE = 16
+GROUPS = ((0, 2), (2, 2), (4, 1), (5, 1))
 
 
 def nn(a, b):
@@ -88,44 +89,48 @@
     def far_copy(p, n, src):
         return remote(far.at[src, p], far.at[src, p], far_s.at[n - 1, p], far_r.at[n - 1, p], y_peer(n))
 
-    def df_copy(p, a, n):
-        block = dfs.at[lax.rem(p, 2), a, lax.rem(y + n, 4)]
-        return remote(block, dfr.at[p, a, n - 1], df_s.at[a, n - 1, p], df_r.at[a, n - 1, p], y_peer(n))
-
-    def a_copy(p):
-        block = part.at[lax.rem(p, 2), ds((1 - core) * HALF, HALF, HALF)]
-        return remote(block, ar.at[p], a_s.at[p], a_r.at[p], sibling)
-
-    def b_copy(p, n):
-        block = bs.at[lax.rem(p, 2), ds(lax.rem(spot + n, PLANE) * PIECE, PIECE, PIECE)]
-        return remote(block, br.at[p, n - 1], b_s.at[p], b_r.at[p], plane_peer(n))
-
-    def b_all(p):
-        block = br.at[p]
-        return remote(block, block, b_s.at[p], b_r.at[p], sibling)
-
-    def y_copy(p, n, src):
-        return remote(yr.at[p, src], yr.at[p, src], y_s.at[n - 1, p], y_r.at[n - 1, p], y_peer(n))
-
-    def g_copy(p, n):
-        block = total.at[p, ds(core * HALF + spot * PIECE, PIECE, PIECE)]
-        return remote(fin.at[p], block, g_s.at[p], g_r.at[p], plane_peer(n))
-
-    def g_all(p):
-        block = total.at[p, 0 : HALF - PIECE]
-        return remote(block, block, g_s.at[p], g_r.at[p], sibling)
-
-    def gl_copy(p):
-        block = total.at[p, ds(core * HALF + spot * PIECE, PIECE, PIECE)]
-        return pltpu.make_async_copy(fin.at[p], block, gl_s.at[p])
-
-    def gc_copy(p, src):
-        block = total.at[p, ds(src * HALF, HALF, HALF)]
-        return remote(block, block, gc_s.at[p], gc_r.at[p], sibling)
-
-    def to_plane(copy, p):
+    def df_copy(p, n):
+        block = dfs.at[lax.rem(p, 2), lax.rem(y + n, 4)]
+        return remote(block, dfr.at[p, n - 1], df_s.at[n - 1, p], df_r.at[n - 1, p], y_peer(n))
+
+    def span(g):
+        return slice(GROUPS[g][0], sum(GROUPS[g]))
+
+    def a_copy(g):
+        block = part.at[span(g), ds((1 - core) * HALF, HALF, HALF)]
+        return remote(block, ar.at[span(g)], a_s.at[g], a_r.at[g], sibling)
+
+    def b_copy(g, n):
+        block = bs.at[span(g), ds(lax.rem(spot + n, PLANE) * PIECE, PIECE, PIECE)]
+        return remote(block, br.at[n - 1, span(g)], b_s.at[g], b_r.at[g], plane_peer(n))
+
+    def b_all(g):
+        block = br.at[:, span(g)]
+        return remote(block, block, b_s.at[g], b_r.at[g], sibling)
+
+    def y_copy(g, n, src):
+        block = yr.at[src, span(g)]
+        return remote(block, block, y_s.at[n - 1, g], y_r.at[n - 1, g], y_peer(n))
+
+    def g_copy(g, n):
+        block = total.at[span(g), ds(core * HALF + spot * PIECE, PIECE, PIECE)]
+        return remote(fin.at[span(g)], block, g_s.at[g], g_r.at[g], plane_peer(n))
+
+    def g_all(g):
+        block = total.at[span(g), 0 : HALF - PIECE]
+        return remote(block, block, g_s.at[g], g_r.at[g], sibling)
+
+    def gl_copy(g):
+        block = total.at[span(g), ds(core * HALF + spot * PIECE, PIECE, PIECE)]
+        return pltpu.make_async_copy(fin.at[span(g)], block, gl_s.at[g])
+
+    def gc_copy(g, src):
+        block = total.at[span(g), ds(src * HALF, HALF, HALF)]
+        return remote(block, block, gc_s.at[g], gc_r.at[g], sibling)
+
+    def to_plane(copy, g):
         def one(n, carry):
-            copy(p, n).start()
+            copy(g, n).start()
             return carry
 
         lax.fori_loop(1, PLANE, one, 0)
@@ -244,10 +249,11 @@
         dfk = (nt(qc[sl], dsf) * LN2).astype(BF)
         dfv = nt(dwc[sl], ef).astype(BF)
         for j in range(4):
-            dfs[slot, a, j, 0] = dfk[:, j * FAR : j * FAR + FAR]
-            dfs[slot, a, j, 1] = dfv[:, j * FAR : j * FAR + FAR]
-        for n in (1, 2, 3):
-            df_copy(i, a, n).start()
+            dfs[slot, j, a, 0] = dfk[:, j * FAR : j * FAR + FAR]
+            dfs[slot, j, a, 1] = dfv[:, j * FAR : j * FAR + FAR]
+        if a == 1:
+            for n in (1, 2, 3):
+                df_copy(i, n).start()
         for b in range(4):
             at = slice(b * FAR, b * FAR + FAR)
             ds_scr[:, at] = e_scr[:, at] * nn(va, t_scr[0, :, at]).astype(BF)
@@ -259,73 +265,77 @@
 
     def weigh(p):
         slot = lax.rem(p, 2)
+        for n in (1, 2, 3):
+            df_copy(p, n).wait()
         for a in range(2):
-            for n in (1, 2, 3):
-                df_copy(p, a, n).wait()
             sl = slice(HEAD * a, HEAD * a + HEAD)
             at = ds((2 * slot + a) * FAR, FAR, FAR)
             for n, dst in ((0, dkT), (1, dvT)):
-                own = dfs[slot, a, y, n].astype(F32)
+                own = dfs[slot, y, a, n].astype(F32)
                 for m in range(3):
-                    own = own + dfr[p, a, m, n].astype(F32)
+                    own = own + dfr[p, m, a, n].astype(F32)
                 dst[p, sl, :] = near[slot, n, sl, :].astype(BF)
                 dst[p, sl, at] = (near[slot, n, sl, at] + own).astype(BF)
         for n, src in enumerate((dqT, dkT, dvT)):
-            part[slot, n * D : n * D + D, :] = nt(xpT[...], src[p]).astype(BF)
+            part[p, n * D : n * D + D, :] = nt(xpT[...], src[p]).astype(BF)
         gout = nn(ctxT[p], cp[...]).astype(BF)
         for t in range(6):
             at = 3 * D + t * 128
-            part[slot, at : at + 128, :] = gout[:, t * 128 : t * 128 + 128]
-        a_copy(p).start()
-
-    def sum_core(p):
-        slot = lax.rem(p, 2)
-        a_copy(p).wait()
-        mine = part[slot, ds(core * HALF, HALF, HALF), :]
-        bs[slot] = (mine.astype(F32) + ar[p].astype(F32)).astype(BF)
-        to_plane(b_copy, p)
-
-    def sum_plane(p):
-        b_all(p).wait()
-        acc = bs[lax.rem(p, 2), ds(spot * PIECE, PIECE, PIECE), :].astype(F32)
-        for n in range(PLANE - 1):
-            acc = acc + br[p, n].astype(F32)
-        yr[p, y] = acc.astype(BF)
-        for n in (1, 2, 3):
-            y_copy(p, n, y).start()
-
-    def sum_y(p):
-        for n in (1, 2, 3):
-            y_copy(p, n, y).wait_send()
-            y_copy(p, n, back(y, n)).wait_recv()
-        acc = yr[p, 0].astype(F32)
-        for n in (1, 2, 3):
-            acc = acc + yr[p, n].astype(F32)
-        fin[p] = acc.astype(BF)
-        gl_copy(p).start()
-        to_plane(g_copy, p)
-
-    def gather(p):
-        gl_copy(p).wait()
-        g_all(p).wait()
-        gc_copy(p, core).start()
-
-    def end(p):
-        gc_copy(p, core).wait_send()
-        gc_copy(p, 1 - core).wait_recv()
-
-    first = ((weigh, 1), (sum_plane, 2), (gather, 3))
-    second = ((sum_core, 1), (sum_y, 2), (end, 3))
+            part[p, at : at + 128, :] = gout[:, t * 128 : t * 128 + 128]
+
+    def send(g):
+        a_copy(g).start()
+
+    def sum_core(g):
+        a_copy(g).wait()
+        for p in range(PAIRS)[span(g)]:
+            mine = part[p, ds(core * HALF, HALF, HALF), :]
+            bs[p] = (mine.astype(F32) + ar[p].astype(F32)).astype(BF)
+        to_plane(b_copy, g)
+
+    def sum_plane(g):
+        b_all(g).wait()
+        for p in range(PAIRS)[span(g)]:
+            acc = bs[p, ds(spot * PIECE, PIECE, PIECE), :].astype(F32)
+            for n in range(PLANE - 1):
+                acc = acc + br[n, p].astype(F32)
+            yr[y, p] = acc.astype(BF)
+        for n in (1, 2, 3):
+            y_copy(g, n, y).start()
+
+    def sum_y(g):
+        for n in (1, 2, 3):
+            y_copy(g, n, y).wait_send()
+            y_copy(g, n, back(y, n)).wait_recv()
+        acc = yr[0, span(g)].astype(F32)
+        for n in (1, 2, 3):
+            acc = acc + yr[n, span(g)].astype(F32)
+        fin[span(g)] = acc.astype(BF)
+        gl_copy(g).start()
+        to_plane(g_copy, g)
+
+    def gather(g):
+        gl_copy(g).wait()
+        g_all(g).wait()
+        gc_copy(g, core).start()
+
+    def end(g):
+        gc_copy(g, core).wait_send()
+        gc_copy(g, 1 - core).wait_recv()
+
+    first = ((2, send, 0), (4, sum_y, 0), (4, send, 1), (5, send, 2), (5, gather, 0))
+    second = ((2, sum_core, 0), (3, sum_plane, 0), (4, sum_core, 1), (5, sum_plane, 1), (5, sum_core, 2))
 
     def step(i, carry):
         prepare(i)
         attend(i, 0)
         pl.when(i < PAIRS - 2)(lambda: send_far(i + 2))
-        for run, lag in first:
-            pl.when(i >= lag)(lambda run=run, lag=lag: run(i - lag))
+        pl.when(i > 0)(lambda: weigh(i - 1))
+        for when, run, g in first:
+            pl.when(i == when)(lambda run=run, g=g: run(g))
         attend(i, 1)
-        for run, lag in second:
-            pl.when(i >= lag)(lambda run=run, lag=lag: run(i - lag))
+        for when, run, g in second:
+            pl.when(i == when)(lambda run=run, g=g: run(g))
         return carry
 
     lax.fori_loop(0, PAIRS, step, 0)
@@ -348,24 +358,27 @@
     att_copy = pltpu.make_async_copy(q, att_hbm, out_sem.at[0])
     grad_copy = pltpu.make_async_copy(k, gx_hbm, out_sem.at[1])
 
-    sum_plane(4)
-    gather(3)
     attended(0)
-    weigh(5)
-    sum_y(4)
-    end(3)
+    weigh(PAIRS - 1)
+    send(3)
+    sum_y(1)
     attended(1)
     att_copy.start()
-    sum_core(5)
-    gather(4)
+    sum_core(3)
+    sum_plane(2)
     patch_grads(0)
-    sum_plane(5)
-    end(4)
+    sum_plane(3)
+    sum_y(2)
+    gather(1)
     patch_grads(1)
     grad_copy.start()
-    sum_y(5)
-    gather(5)
-    end(5)
+    sum_y(3)
+    gather(2)
+    end(0)
+    end(1)
+    gather(3)
+    end(2)
+    end(3)
     att_copy.wait()
     grad_copy.wait()
     for p in range(PAIRS):
@@ -376,7 +389,7 @@
 def sublayer(info, x, cot, wq, wk, wv, wo):
     anywhere = pl.BlockSpec(memory_space=pl.ANY)
     dma = pltpu.SemaphoreType.DMA
-    three, each = dma((3, PAIRS)), dma((PAIRS,))
+    three, each, group = dma((3, PAIRS)), dma((len(GROUPS),)), dma((3, len(GROUPS)))
     scratch = [
         *[pltpu.VMEM((D, D), BF)] * 4,
         pltpu.VMEM((D, ROWS), BF),
@@ -389,16 +402,16 @@
         pltpu.VMEM((9, 128, ROWS), BF),
         pltpu.VMEM((HEAD + 16, ROWS), F32),
         pltpu.VMEM((2, 2, 128, ROWS), F32),
-        pltpu.VMEM((2, 2, 4, 2, HEAD, FAR), BF),
-        pltpu.VMEM((PAIRS, 2, 3, 2, HEAD, FAR), BF),
-        pltpu.VMEM((2, PART, 128), BF),
+        pltpu.VMEM((2, 4, 2, 2, HEAD, FAR), BF),
+        pltpu.VMEM((PAIRS, 3, 2, 2, HEAD, FAR), BF),
+        pltpu.VMEM((PAIRS, PART, 128), BF),
         pltpu.VMEM((PAIRS, HALF, 128), BF),
-        pltpu.VMEM((2, HALF, 128), BF),
-        pltpu.VMEM((PAIRS, PLANE - 1, PIECE, 128), BF),
-        pltpu.VMEM((PAIRS, 4, PIECE, 128), BF),
+        pltpu.VMEM((PAIRS, HALF, 128), BF),
+        pltpu.VMEM((PLANE - 1, PAIRS, PIECE, 128), BF),
+        pltpu.VMEM((4, PAIRS, PIECE, 128), BF),
         pltpu.VMEM((PAIRS, PIECE, 128), BF),
         dma((6,)),
-        three, three, dma((2, 3, PAIRS)), dma((2, 3, PAIRS)), each, each, each, each, three, three,
+        three, three, three, three, each, each, each, each, group, group,
         each, each, each, each, each, dma((2,)),
     ]
     return pl.pallas_call(
@@ -420,21 +433,23 @@
 def assemble_kernel(att, gx, total, att_out, gx_out, gq, gk, gv, go):
     att_out[...] = att[...]
     gx_out[...] = gx[...]
-    for n, ref in enumerate((gq, gk, gv)):
-        ref[...] = total[0, n * D : n * D + D, :]
-    for t in range(PAIRS):
-        go[:, t * 128 : t * 128 + 128] = total[0, 3 * D + t * 128 : 3 * D + t * 128 + 128, :]
+    for p in range(2):
+        at = slice(p * 128, p * 128 + 128)
+        for n, ref in enumerate((gq, gk, gv)):
+            ref[:, at] = total[p, n * D : n * D + D, :]
+        for t in range(PAIRS):
+            go[at, t * 128 : t * 128 + 128] = total[p, 3 * D + t * 128 : 3 * D + t * 128 + 128, :]
 
 
 def assemble(att, gx, total):
     rows, square = jax.ShapeDtypeStruct((ROWS, D), BF), jax.ShapeDtypeStruct((D, D), BF)
-    wide = pl.BlockSpec((ROWS, 128), lambda p: (0, p))
-    column = pl.BlockSpec((D, 128), lambda p: (0, p))
+    wide = pl.BlockSpec((ROWS, 256), lambda p: (0, p))
+    column = pl.BlockSpec((D, 256), lambda p: (0, p))
     return pl.pallas_call(
         assemble_kernel,
-        grid=(PAIRS,),
-        in_specs=[wide, wide, pl.BlockSpec((1, PART, 128), lambda p: (p, 0, 0))],
-        out_specs=[wide, wide, column, column, column, pl.BlockSpec((128, D), lambda p: (p, 0))],
+        grid=(PAIRS // 2,),
+        in_specs=[wide, wide, pl.BlockSpec((2, PART, 128), lambda p: (p, 0, 0))],
+        out_specs=[wide, wide, column, column, column, pl.BlockSpec((256, D), lambda p: (p, 0))],
         out_shape=[rows, rows, square, square, square, square],
         compiler_params=pltpu.CompilerParams(vmem_limit_bytes=VMEM_LIMIT),
     )(att, gx, total)

time: 154 us -> 144 us (0.935)
  Pallas kernels: 153 us -> 142 us
    pallas_call x1, Pallas kernels: 145 us -> 134 us  [sublayer(): pl.pallas_call(kernel, in_specs=[pl.BlockSpec(memory_space=pltpu.SMEM)] +...]
where the time goes in v4:
time: 144 us; the launch traced here: 143 us
  Pallas kernels  142 us (99%)
    pallas_call x1, Pallas kernels, sublayer(): pl.pallas_call(kernel, in_specs=[pl.BlockSpec(memory_space=pltpu.SMEM)] +...  134 us
    pallas_call x1, Pallas kernels, assemble(): pl.pallas_call(assemble_kernel, grid=(PAIRS // 2,), in_specs=[wide, wide,...  7.67 us

profile of v4, /device:TPU:1, one launch (start us, length us, event | category | flops | bytes accessed | tf_op | source)
XLA Modules:
  0.0 143.4 jit_solution(6105239993481949011)
XLA Ops:
  1.3 134.4 %shard_map.118 = (bf16[1024,768]{1,0:T(8,128)(2,1)}, bf16[1024,768]{1,0:T(8,128)(2,1)}, bf16[6,3072,128]{2,1,0:T(8,128)(2,1)}) custom-call(s32[1]{0:T(128)S(6)} %copy.13.info, bf16[1024,768]{1,0:T(8,128)(2,1)} %bitcast.4, bf16[1024,768]{1,0:T(8,128)(2,1)} %bitcast.5, bf16[768,768]{1,0:T(8,128)(2,1)} %wq_hbm.1, bf16[768,768]{1,0:T(8,128)(2,1)} %wk_hbm.1, ...), custom_call_target="tpu_custom_call" | custom-call | tf_op jit(solution)/shard_map/pallas_call | solution.py:417
  135.7 7.7 %shard_map.119 = (bf16[1024,768]{1,0:T(8,128)(2,1)}, bf16[1024,768]{1,0:T(8,128)(2,1)}, bf16[768,768]{1,0:T(8,128)(2,1)}, bf16[768,768]{1,0:T(8,128)(2,1)}, bf16...) custom-call(bf16[1024,768]{1,0:T(8,128)(2,1)} %get-tuple-element.15.att, bf16[1024,768]{1,0:T(8,128)(2,1)} %get-tuple-element.16.gx, ...), custom_call_target="tpu_custom_call" | custom-call | tf_op jit(solution)/shard_map/pallas_call | solution.py:448

commit v5 on v4

--- a/solution.py
+++ b/solution.py
@@ -129,11 +129,8 @@
         return remote(block, block, gc_s.at[g], gc_r.at[g], sibling)
 
     def to_plane(copy, g):
-        def one(n, carry):
+        for n in range(1, PLANE):
             copy(g, n).start()
-            return carry
-
-        lax.fori_loop(1, PLANE, one, 0)
 
     def back(index, n):
         return lax.rem(index + 4 - n, 4)
@@ -265,6 +262,11 @@
 
     def weigh(p):
         slot = lax.rem(p, 2)
+        part[p, 0:D, :] = nt(xpT[...], dqT[p]).astype(BF)
+        gout = nn(ctxT[p], cp[...]).astype(BF)
+        for t in range(6):
+            at = 3 * D + t * 128
+            part[p, at : at + 128, :] = gout[:, t * 128 : t * 128 + 128]
         for n in (1, 2, 3):
             df_copy(p, n).wait()
         for a in range(2):
@@ -276,12 +278,8 @@
                     own = own + dfr[p, m, a, n].astype(F32)
                 dst[p, sl, :] = near[slot, n, sl, :].astype(BF)
                 dst[p, sl, at] = (near[slot, n, sl, at] + own).astype(BF)
-        for n, src in enumerate((dqT, dkT, dvT)):
+        for n, src in ((1, dkT), (2, dvT)):
             part[p, n * D : n * D + D, :] = nt(xpT[...], src[p]).astype(BF)
-        gout = nn(ctxT[p], cp[...]).astype(BF)
-        for t in range(6):
-            at = 3 * D + t * 128
-            part[p, at : at + 128, :] = gout[:, t * 128 : t * 128 + 128]
 
     def send(g):
         a_copy(g).start()
@@ -433,7 +431,7 @@
 def assemble_kernel(att, gx, total, att_out, gx_out, gq, gk, gv, go):
     att_out[...] = att[...]
     gx_out[...] = gx[...]
-    for p in range(2):
+    for p in range(3):
         at = slice(p * 128, p * 128 + 128)
         for n, ref in enumerate((gq, gk, gv)):
             ref[:, at] = total[p, n * D : n * D + D, :]
@@ -443,13 +441,13 @@
 
 def assemble(att, gx, total):
     rows, square = jax.ShapeDtypeStruct((ROWS, D), BF), jax.ShapeDtypeStruct((D, D), BF)
-    wide = pl.BlockSpec((ROWS, 256), lambda p: (0, p))
-    column = pl.BlockSpec((D, 256), lambda p: (0, p))
+    wide = pl.BlockSpec((ROWS // 2, D), lambda p: (p, 0))
+    column = pl.BlockSpec((D, 384), lambda p: (0, p))
     return pl.pallas_call(
         assemble_kernel,
-        grid=(PAIRS // 2,),
-        in_specs=[wide, wide, pl.BlockSpec((2, PART, 128), lambda p: (p, 0, 0))],
-        out_specs=[wide, wide, column, column, column, pl.BlockSpec((256, D), lambda p: (p, 0))],
+        grid=(2,),
+        in_specs=[wide, wide, pl.BlockSpec((3, PART, 128), lambda p: (p, 0, 0))],
+        out_specs=[wide, wide, column, column, column, pl.BlockSpec((384, D), lambda p: (p, 0))],
         out_shape=[rows, rows, square, square, square, square],
         compiler_params=pltpu.CompilerParams(vmem_limit_bytes=VMEM_LIMIT),
     )(att, gx, total)

time: 144 us -> 140 us (0.972)
  Pallas kernels: 142 us -> 139 us
    pallas_call x1, Pallas kernels: 7.67 us -> 5.82 us  [assemble(): pl.pallas_call(assemble_kernel, grid=(2,), in_specs=[wide, wide, pl.Block...]
where the time goes in v5:
time: 140 us
  Pallas kernels  139 us (99%)
    pallas_call x1, Pallas kernels, sublayer(): pl.pallas_call(kernel, in_specs=[pl.BlockSpec(memory_space=pltpu.SMEM)] +...  133 us
    pallas_call x1, Pallas kernels, assemble(): pl.pallas_call(assemble_kernel, grid=(2,), in_specs=[wide, wide, pl.Block...  5.82 us

profile of v5, /device:TPU:1, one launch (start us, length us, event | category | flops | bytes accessed | tf_op | source)
XLA Modules:
  0.0 140.2 jit_solution(7974676116183440916)
XLA Ops:
  1.3 133.1 %shard_map.118 = (bf16[1024,768]{1,0:T(8,128)(2,1)}, bf16[1024,768]{1,0:T(8,128)(2,1)}, bf16[6,3072,128]{2,1,0:T(8,128)(2,1)}) custom-call(s32[1]{0:T(128)S(6)} %copy.13.info, bf16[1024,768]{1,0:T(8,128)(2,1)} %bitcast.4, bf16[1024,768]{1,0:T(8,128)(2,1)} %bitcast.5, bf16[768,768]{1,0:T(8,128)(2,1)} %wq_hbm.1, bf16[768,768]{1,0:T(8,128)(2,1)} %wk_hbm.1, ...), custom_call_target="tpu_custom_call" | custom-call | tf_op jit(solution)/shard_map/pallas_call | solution.py:415
  134.3 5.8 %shard_map.119 = (bf16[1024,768]{1,0:T(8,128)(2,1)}, bf16[1024,768]{1,0:T(8,128)(2,1)}, bf16[768,768]{1,0:T(8,128)(2,1)}, bf16[768,768]{1,0:T(8,128)(2,1)}, bf16...) custom-call(bf16[1024,768]{1,0:T(8,128)(2,1)} %get-tuple-element.15.att, bf16[1024,768]{1,0:T(8,128)(2,1)} %get-tuple-element.16.gx, ...), custom_call_target="tpu_custom_call" | custom-call | tf_op jit(solution)/shard_map/pallas_call | solution.py:446
